TPU v7x, 256 devices: a whole 4x4x8 slice. The times are simulated.
256 devices in a mesh: row: 8 (over x, core), col: 32 (over y, z).
Axes of the slice: x: 4, y: 4, z: 8, core: 2. Of those that a mesh axis runs over, the one named last changes fastest.
Arguments:
- hamiltonian: bfloat16 [7, 16, 32, 128, 128], P(None, 'row', 'col'), may hold values from -0.09375 to 0.09375
- term_prev: bfloat16 [7, 16, 32, 128, 128], P(None, 'row', 'col'), may hold values from -6 to 6
- term_now: bfloat16 [7, 16, 32, 128, 128], P(None, 'row', 'col'), may hold values from -6 to 6
- pattern: int32 [7, 16, 32], P(None, 'row', 'col'), may hold values from 0 to 1, as said below
- weights: float32 [12], replicated, may hold values from 0.5 to 1.5
Outputs:
- density: float32 [7, 16, 32, 128, 128], P(None, 'row', 'col')
- term_before: bfloat16 [7, 16, 32, 128, 128], P(None, 'row', 'col')
- term_last: bfloat16 [7, 16, 32, 128, 128], P(None, 'row', 'col')
Inputs may be any that keep to these rules, and one draw needn't show every extreme that they name: `pattern`: the offset-zero entries (index 3) are always 1; about three quarters of the others are 1.
All inputs are finite; a program needn't handle non-finite values.
Results may differ from a plain program's by a relative error of at most 0.011.
Values may be sent and summed in bfloat16 or wider, within the bound.
No kernel may reach another device: no remote copies, remote signals or barrier semaphores. Data moves between devices by JAX's collectives and lax.ppermute only.
A program may use at most 64 MiB of HBM per device.

v0:
```python
import jax
import jax.numpy as jnp
from jax import lax
from jax.sharding import PartitionSpec as P

BAND = 3
TERMS = 12


def shifted(array, axis, by):
    peers = lax.axis_size(axis)
    return lax.ppermute(array, axis, [(i, (i + by) % peers) for i in range(peers)])


def band_times(term_band, neighbours, live_mask):
    accum = jnp.zeros(term_band.shape, jnp.float32)
    for shift_by in range(-BAND, BAND + 1):
        slab, first_b = neighbours[shift_by]
        low_b = max(-BAND, -BAND - shift_by)
        high_b = min(BAND, BAND - shift_by)
        partial_sum = jnp.einsum(
            "qxy,bqyz->bqxz",
            term_band[shift_by + BAND],
            slab[low_b + BAND - first_b : high_b + BAND - first_b + 1],
            preferred_element_type=jnp.float32,
        )
        accum = accum.at[low_b + shift_by + BAND : high_b + shift_by + BAND + 1].add(partial_sum)
    return accum * live_mask


def body(hamiltonian, term_prev, term_now, pattern, weights):
    out_shape = hamiltonian.shape
    offsets = hamiltonian.shape[0]
    rows_here = hamiltonian.shape[1]
    block = hamiltonian.shape[3]
    band_shape = (offsets, rows_here, block, block)
    live_mask = pattern.reshape(offsets, rows_here, 1, 1).astype(jnp.float32)
    ham_band = (hamiltonian.reshape(band_shape) * live_mask).astype(jnp.bfloat16)
    older = term_prev.reshape(band_shape) * live_mask
    newer = (term_now.reshape(band_shape) * live_mask).astype(jnp.bfloat16)
    col_count = lax.axis_size("col")
    col_index = lax.axis_index("col")
    neighbours = {0: (ham_band, 0)}
    for shift_by in range(-BAND, BAND + 1):
        if shift_by != 0:
            first_b = 0
            received = shifted(ham_band, "col", -shift_by)
            edge_rows = received[:, :1] if shift_by > 0 else received[:, rows_here - 1 :]
            rim_rows = shifted(edge_rows, "row", -1 if shift_by > 0 else 1)
            if shift_by > 0:
                carried = jnp.concatenate([received[:, 1:], rim_rows], axis=1)
            else:
                carried = jnp.concatenate([rim_rows, received[:, : rows_here - 1]], axis=1)
            if shift_by > 0:
                wraps = col_index + shift_by >= col_count
            else:
                wraps = col_index + shift_by < 0
            neighbours[shift_by] = (jnp.where(wraps, carried, received), first_b)
    density = jnp.zeros(band_shape, jnp.float32)
    for step in range(TERMS):
        product = band_times(newer, neighbours, live_mask)
        following = 2.0 * product - older
        density = density + weights[step] * following
        older = newer.astype(jnp.float32)
        newer = following.astype(jnp.bfloat16)
    return (
        density.reshape(out_shape),
        older.astype(jnp.bfloat16).reshape(out_shape),
        newer.reshape(out_shape),
    )


def solution(mesh):
    placed = (
        P(None, "row", "col", None, None),
        P(None, "row", "col", None, None),
        P(None, "row", "col", None, None),
        P(None, "row", "col"),
        P(),
    )
    return jax.shard_map(
        body,
        mesh=mesh,
        in_specs=placed,
        out_specs=(
            P(None, "row", "col", None, None),
            P(None, "row", "col", None, None),
            P(None, "row", "col", None, None),
        ),
        check_vma=False,
    )
```

profile of v0, /device:TPU:1, one launch (start us, length us, event | category | flops | bytes accessed | tf_op | source)
XLA Modules:
  0.0 240.7 jit_solution(10116918652487304361)
XLA Ops:
  2.9 5.3 %collective-permute-start = (bf16[7,2,128,128]{3,2,1,0:T(8,128)(2,1)S(1)}, bf16[7,2,128,128]{3,2,1,0:T(8,128)(2,1)S(1)}, u32[]{:S(2)}, u32[]{:S(2)}) collective-permute-start(bf16[7,2,128,128]{3,2,1,0:T(8,128)(2,1)S(1)} %get-tuple-element.1123), channel_id=1, source_target_pairs={{0,3},{1,4},{2,5},{3,6},{4,7},{5,8},{6,9},{7,10},{8,11},{9,12},{10... | collective-permute-start | bytes 1376264 | tf_op jit(solution)/shard_map/ppermute | solution.py:12
  8.1 3.3 %collective-permute-start.2 = (bf16[7,2,128,128]{3,2,1,0:T(8,128)(2,1)S(1)}, bf16[7,2,128,128]{3,2,1,0:T(8,128)(2,1)S(1)}, u32[]{:S(2)}, u32[]{:S(2)}) collective-permute-start(bf16[7,2,128,128]{3,2,1,0:T(8,128)(2,1)S(1)} %get-tuple-element.1123), channel_id=1, source_target_pairs={{0,2},{1,3},{2,4},{3,5},{4,6},{5,7},{6,8},{7,9},{8,10},{9,11},{10,... | collective-permute-start | bytes 1376264 | tf_op jit(solution)/shard_map/ppermute | solution.py:12
  12.2 4.0 %collective-permute-start.6 = (bf16[7,2,128,128]{3,2,1,0:T(8,128)(2,1)S(1)}, bf16[7,2,128,128]{3,2,1,0:T(8,128)(2,1)S(1)}, u32[]{:S(2)}, u32[]{:S(2)}) collective-permute-start(bf16[7,2,128,128]{3,2,1,0:T(8,128)(2,1)S(1)} %get-tuple-element.1123), channel_id=1, source_target_pairs={{0,31},{1,0},{2,1},{3,2},{4,3},{5,4},{6,5},{7,6},{8,7},{9,8},{10,9... | collective-permute-start | bytes 1376264 | tf_op jit(solution)/shard_map/ppermute | solution.py:12
  18.0 20.0 %collective-permute-done = bf16[7,2,128,128]{3,2,1,0:T(8,128)(2,1)S(1)} collective-permute-done((bf16[7,2,128,128]{3,2,1,0:T(8,128)(2,1)S(1)}, bf16[7,2,128,128]{3,2,1,0:T(8,128)(2,1)S(1)}, u32[]{:S(2)}, u32[]{:S(2)}) %collective-permute-start) | collective-permute-done | bytes 458784 | tf_op jit(solution)/shard_map/ppermute | solution.py:12
  38.0 6.3 %collective-permute-start.10 = (bf16[7,2,128,128]{3,2,1,0:T(8,128)(2,1)S(1)}, bf16[7,2,128,128]{3,2,1,0:T(8,128)(2,1)S(1)}, u32[]{:S(2)}, u32[]{:S(2)}) collective-permute-start(bf16[7,2,128,128]{3,2,1,0:T(8,128)(2,1)S(1)} %get-tuple-element.1123), channel_id=1, source_target_pairs={{0,29},{1,30},{2,31},{3,0},{4,1},{5,2},{6,3},{7,4},{8,5},{9,6},{10... | collective-permute-start | bytes 1376264 | tf_op jit(solution)/shard_map/ppermute | solution.py:12
  44.4 15.2 %collective-permute-done.2 = bf16[7,2,128,128]{3,2,1,0:T(8,128)(2,1)S(1)} collective-permute-done((bf16[7,2,128,128]{3,2,1,0:T(8,128)(2,1)S(1)}, bf16[7,2,128,128]{3,2,1,0:T(8,128)(2,1)S(1)}, u32[]{:S(2)}, u32[]{:S(2)}) %collective-permute-start.2) | collective-permute-done | bytes 458784 | tf_op jit(solution)/shard_map/ppermute | solution.py:12
  59.5 4.6 %collective-permute-start.1 = (bf16[7,1,128,128]{3,2,1,0:T(8,128)(2,1)S(1)}, bf16[7,1,128,128]{3,2,1,0:T(8,128)(2,1)S(1)}, u32[]{:S(2)}, u32[]{:S(2)}) collective-permute-start(bf16[7,1,128,128]{3,2,1,0:T(8,128)(2,1)S(1)} %get-tuple-element.1120), channel_id=1, source_target_pairs={{0,32},{32,64},{64,96},{96,128},{128,160},{160,192},{192,224},{224... | collective-permute-start | bytes 688136 | tf_op jit(solution)/shard_map/ppermute | solution.py:12
  64.1 7.5 %collective-permute-done.4 = bf16[7,2,128,128]{3,2,1,0:T(8,128)(2,1)S(1)} collective-permute-done((bf16[7,2,128,128]{3,2,1,0:T(8,128)(2,1)S(1)}, bf16[7,2,128,128]{3,2,1,0:T(8,128)(2,1)S(1)}, u32[]{:S(2)}, u32[]{:S(2)}) %collective-permute-start.4) | collective-permute-done | bytes 458784 | tf_op jit(solution)/shard_map/ppermute | solution.py:12
  92.6 2.3 fusion.41
  94.9 2.4 fusion.2
  106.5 2.3 fusion.38
  108.7 2.4 %fusion.3 = f32[7,2,128,128]{3,2,1,0:T(8,128)} fusion(f32[7,2,128,128]{3,2,1,0:T(8,128)} %fusion.38, bf16[7,2,128,128]{3,2,1,0:T(8,128)(2,1)S(1)} %get-tuple-element.1123, bf16[7,2,128,128]{3,2,1,0:T(8,128)(2,1)S(1)} %fusion.76), kind=kOutput, calls=%fused_computation.15 | convolution fusion | flops 58949632 | bytes 2359296 | tf_op jit(solution)/shard_map/qxy,bqyz->bqxz/dot_general | solution.py:21
  120.5 2.3 fusion.35
  122.8 2.4 fusion.4
  134.4 2.3 fusion.32
  136.7 2.4 fusion.5
  148.2 2.3 fusion.29
  150.5 2.4 fusion.6
  160.0 2.2 fusion.57
  162.2 2.5 %fusion.26 = f32[7,2,128,128]{3,2,1,0:T(8,128)} fusion(f32[7,2,128,128]{3,2,1,0:T(8,128)} %fusion.57, bf16[6,2,128,128]{3,2,1,0:T(8,128)(2,1)S(1)} %slice_select_fusion.1, bf16[7,2,128,128]{3,2,1,0:T(8,128)(2,1)S(1)} %fusion.80), kind=kOutput, calls=%fused_computation.48 | convolution fusion | flops 50528256 | bytes 2031616 | tf_op jit(solution)/shard_map/qxy,bqyz->bqxz/dot_general | solution.py:21
  164.7 2.4 fusion.7
  176.3 2.3 fusion.23
  178.6 2.4 %fusion.8 = f32[7,2,128,128]{3,2,1,0:T(8,128)} fusion(f32[7,2,128,128]{3,2,1,0:T(8,128)} %fusion.23, bf16[7,2,128,128]{3,2,1,0:T(8,128)(2,1)S(1)} %get-tuple-element.1123, bf16[7,2,128,128]{3,2,1,0:T(8,128)(2,1)S(1)} %fusion.81), kind=kOutput, calls=%fused_computation.20 | convolution fusion | flops 58949632 | bytes 2359296 | tf_op jit(solution)/shard_map/qxy,bqyz->bqxz/dot_general | solution.py:21
  190.2 2.3 fusion.20
  192.4 2.4 fusion.9
  202.0 2.2 fusion.51
  204.2 2.3 fusion.17
  206.6 2.4 fusion.10
  218.2 2.3 fusion.14
  220.5 2.4 %fusion.11 = f32[7,2,128,128]{3,2,1,0:T(8,128)} fusion(f32[7,2,128,128]{3,2,1,0:T(8,128)} %fusion.14, bf16[7,2,128,128]{3,2,1,0:T(8,128)(2,1)S(1)} %get-tuple-element.1123, bf16[7,2,128,128]{3,2,1,0:T(8,128)(2,1)S(1)} %fusion.84), kind=kOutput, calls=%fused_computation.23 | convolution fusion | flops 58949632 | bytes 2359296 | tf_op jit(solution)/shard_map/qxy,bqyz->bqxz/dot_general | solution.py:21
  227.6 2.3 fusion.99
  230.0 10.7 %add_bitcast_fusion = f32[7,2,1,128,128]{4,3,2,1,0:T(8,128)} fusion(f32[7,2,128,128]{3,2,1,0:T(8,128)S(1)} %fusion.96, bf16[7,2,128,128]{3,2,1,0:T(8,128)(2,1)S(1)} %fusion.98, f32[7,2,128,128]{3,2,1,0:T(8,128)S(1)} %copy-done.1, bf16[7,2,128,128]{3,2,1,0:T(8,128)(2,1)S(1)} %fusion.75, f32[7,2,128,128]{3,2,1,0:T(8,128)S(1)} %copy-done.2, ...), kind=kLoop, calls=%fused_computation.162 | loop fusion | flops 17203200 | bytes 17432680
  (175 shorter events, 108.9 us)
Async XLA Ops:
  2.9 76.8 %copy-start.12 = (bf16[7,2,128,128]{3,2,1,0:T(8,128)(2,1)}, bf16[7,2,128,128]{3,2,1,0:T(8,128)(2,1)S(1)}, u32[]{:S(2)}) copy-start(bf16[7,2,128,128]{3,2,1,0:T(8,128)(2,1)S(1)} %get-tuple-element.1122) | copy-start | bytes 1376260
  2.9 35.1 %collective-permute-start = (bf16[7,2,128,128]{3,2,1,0:T(8,128)(2,1)S(1)}, bf16[7,2,128,128]{3,2,1,0:T(8,128)(2,1)S(1)}, u32[]{:S(2)}, u32[]{:S(2)}) collective-permute-start(bf16[7,2,128,128]{3,2,1,0:T(8,128)(2,1)S(1)} %get-tuple-element.1123), channel_id=1, source_target_pairs={{0,3},{1,4},{2,5},{3,6},{4,7},{5,8},{6,9},{7,10},{8,11},{9,12},{10... | collective-permute-start | bytes 1376264 | tf_op jit(solution)/shard_map/ppermute | solution.py:12
  8.1 51.4 %collective-permute-start.2 = (bf16[7,2,128,128]{3,2,1,0:T(8,128)(2,1)S(1)}, bf16[7,2,128,128]{3,2,1,0:T(8,128)(2,1)S(1)}, u32[]{:S(2)}, u32[]{:S(2)}) collective-permute-start(bf16[7,2,128,128]{3,2,1,0:T(8,128)(2,1)S(1)} %get-tuple-element.1123), channel_id=1, source_target_pairs={{0,2},{1,3},{2,4},{3,5},{4,6},{5,7},{6,8},{7,9},{8,10},{9,11},{10,... | collective-permute-start | bytes 1376264 | tf_op jit(solution)/shard_map/ppermute | solution.py:12
  11.4 60.2 %collective-permute-start.4 = (bf16[7,2,128,128]{3,2,1,0:T(8,128)(2,1)S(1)}, bf16[7,2,128,128]{3,2,1,0:T(8,128)(2,1)S(1)}, u32[]{:S(2)}, u32[]{:S(2)}) collective-permute-start(bf16[7,2,128,128]{3,2,1,0:T(8,128)(2,1)S(1)} %get-tuple-element.1123), channel_id=1, source_target_pairs={{0,1},{1,2},{2,3},{3,4},{4,5},{5,6},{6,7},{7,8},{8,9},{9,10},{10,1... | collective-permute-start | bytes 1376264 | tf_op jit(solution)/shard_map/ppermute | solution.py:12
  12.2 61.5 %collective-permute-start.6 = (bf16[7,2,128,128]{3,2,1,0:T(8,128)(2,1)S(1)}, bf16[7,2,128,128]{3,2,1,0:T(8,128)(2,1)S(1)}, u32[]{:S(2)}, u32[]{:S(2)}) collective-permute-start(bf16[7,2,128,128]{3,2,1,0:T(8,128)(2,1)S(1)} %get-tuple-element.1123), channel_id=1, source_target_pairs={{0,31},{1,0},{2,1},{3,2},{4,3},{5,4},{6,5},{7,6},{8,7},{9,8},{10,9... | collective-permute-start | bytes 1376264 | tf_op jit(solution)/shard_map/ppermute | solution.py:12
  16.2 58.3 %collective-permute-start.8 = (bf16[7,2,128,128]{3,2,1,0:T(8,128)(2,1)S(1)}, bf16[7,2,128,128]{3,2,1,0:T(8,128)(2,1)S(1)}, u32[]{:S(2)}, u32[]{:S(2)}) collective-permute-start(bf16[7,2,128,128]{3,2,1,0:T(8,128)(2,1)S(1)} %get-tuple-element.1123), channel_id=1, source_target_pairs={{0,30},{1,31},{2,0},{3,1},{4,2},{5,3},{6,4},{7,5},{8,6},{9,7},{10,... | collective-permute-start | bytes 1376264 | tf_op jit(solution)/shard_map/ppermute | solution.py:12
  38.0 37.3 %collective-permute-start.10 = (bf16[7,2,128,128]{3,2,1,0:T(8,128)(2,1)S(1)}, bf16[7,2,128,128]{3,2,1,0:T(8,128)(2,1)S(1)}, u32[]{:S(2)}, u32[]{:S(2)}) collective-permute-start(bf16[7,2,128,128]{3,2,1,0:T(8,128)(2,1)S(1)} %get-tuple-element.1123), channel_id=1, source_target_pairs={{0,29},{1,30},{2,31},{3,0},{4,1},{5,2},{6,3},{7,4},{8,5},{9,6},{10... | collective-permute-start | bytes 1376264 | tf_op jit(solution)/shard_map/ppermute | solution.py:12
  59.5 4.6 %copy-start.20 = (bf16[7,2,128,128]{3,2,1,0:T(8,128)(2,1)}, bf16[7,2,128,128]{3,2,1,0:T(8,128)(2,1)S(1)}, u32[]{:S(2)}) copy-start(bf16[7,2,128,128]{3,2,1,0:T(8,128)(2,1)S(1)} %collective-permute-done.2) | copy-start | bytes 1376260
  59.5 16.9 %collective-permute-start.1 = (bf16[7,1,128,128]{3,2,1,0:T(8,128)(2,1)S(1)}, bf16[7,1,128,128]{3,2,1,0:T(8,128)(2,1)S(1)}, u32[]{:S(2)}, u32[]{:S(2)}) collective-permute-start(bf16[7,1,128,128]{3,2,1,0:T(8,128)(2,1)S(1)} %get-tuple-element.1120), channel_id=1, source_target_pairs={{0,32},{32,64},{64,96},{96,128},{128,160},{160,192},{192,224},{224... | collective-permute-start | bytes 688136 | tf_op jit(solution)/shard_map/ppermute | solution.py:12
  71.7 2.1 copy-start.16
  71.7 5.9 %collective-permute-start.3 = (bf16[7,1,128,128]{3,2,1,0:T(8,128)(2,1)S(1)}, bf16[7,1,128,128]{3,2,1,0:T(8,128)(2,1)S(1)}, u32[]{:S(2)}, u32[]{:S(2)}) collective-permute-start(bf16[7,1,128,128]{3,2,1,0:T(8,128)(2,1)S(1)} %get-tuple-element.1118), channel_id=1, source_target_pairs={{0,32},{32,64},{64,96},{96,128},{128,160},{160,192},{192,224},{224... | collective-permute-start | bytes 688136 | tf_op jit(solution)/shard_map/ppermute | solution.py:12
  73.7 5.4 %collective-permute-start.5 = (bf16[7,1,128,128]{3,2,1,0:T(8,128)(2,1)S(1)}, bf16[7,1,128,128]{3,2,1,0:T(8,128)(2,1)S(1)}, u32[]{:S(2)}, u32[]{:S(2)}) collective-permute-start(bf16[7,1,128,128]{3,2,1,0:T(8,128)(2,1)S(1)} %get-tuple-element.1116), channel_id=1, source_target_pairs={{0,32},{32,64},{64,96},{96,128},{128,160},{160,192},{192,224},{224... | collective-permute-start | bytes 688136 | tf_op jit(solution)/shard_map/ppermute | solution.py:12
  74.5 6.6 %collective-permute-start.7 = (bf16[7,1,128,128]{3,2,1,0:T(8,128)(2,1)S(1)}, bf16[7,1,128,128]{3,2,1,0:T(8,128)(2,1)S(1)}, u32[]{:S(2)}, u32[]{:S(2)}) collective-permute-start(bf16[7,1,128,128]{3,2,1,0:T(8,128)(2,1)S(1)} %get-tuple-element.1115), channel_id=1, source_target_pairs={{0,224},{32,0},{64,32},{96,64},{128,96},{160,128},{192,160},{224,1... | collective-permute-start | bytes 688136 | tf_op jit(solution)/shard_map/ppermute | solution.py:12
  75.3 7.1 %collective-permute-start.9 = (bf16[7,1,128,128]{3,2,1,0:T(8,128)(2,1)S(1)}, bf16[7,1,128,128]{3,2,1,0:T(8,128)(2,1)S(1)}, u32[]{:S(2)}, u32[]{:S(2)}) collective-permute-start(bf16[7,1,128,128]{3,2,1,0:T(8,128)(2,1)S(1)} %get-tuple-element.1113), channel_id=1, source_target_pairs={{0,224},{32,0},{64,32},{96,64},{128,96},{160,128},{192,160},{224,1... | collective-permute-start | bytes 688136 | tf_op jit(solution)/shard_map/ppermute | solution.py:12
  76.5 8.4 %collective-permute-start.11 = (bf16[7,1,128,128]{3,2,1,0:T(8,128)(2,1)S(1)}, bf16[7,1,128,128]{3,2,1,0:T(8,128)(2,1)S(1)}, u32[]{:S(2)}, u32[]{:S(2)}) collective-permute-start(bf16[7,1,128,128]{3,2,1,0:T(8,128)(2,1)S(1)} %get-tuple-element.1111), channel_id=1, source_target_pairs={{0,224},{32,0},{64,32},{96,64},{128,96},{160,128},{192,160},{224,1... | collective-permute-start | bytes 688136 | tf_op jit(solution)/shard_map/ppermute | solution.py:12
  77.5 1.0 copy-start.21
  78.6 1.0 copy-start.17
  79.9 1.2 copy-start.15
  82.3 1.0 copy-start.19
  84.9 1.1 copy-start.11
  88.0 1.0 copy-start.10
  214.8 11.8 %copy-start.13 = (bf16[7,2,128,128]{3,2,1,0:T(8,128)(2,1)}, bf16[7,2,128,128]{3,2,1,0:T(8,128)(2,1)S(1)}, u32[]{:S(2)}) copy-start(bf16[7,2,128,128]{3,2,1,0:T(8,128)(2,1)S(1)} %fusion.84) | copy-start | bytes 1376260
  222.9 7.0 %copy-start.7 = (f32[7,2,128,128]{3,2,1,0:T(8,128)S(1)}, f32[7,2,128,128]{3,2,1,0:T(8,128)}, u32[]{:S(2)}) copy-start(f32[7,2,128,128]{3,2,1,0:T(8,128)} %fusion.89) | copy-start | bytes 2752516
  222.9 7.0 %copy-start.8 = (f32[7,2,128,128]{3,2,1,0:T(8,128)S(1)}, f32[7,2,128,128]{3,2,1,0:T(8,128)}, u32[]{:S(2)}) copy-start(f32[7,2,128,128]{3,2,1,0:T(8,128)} %fusion.88) | copy-start | bytes 2752516
  222.9 7.0 %copy-start.9 = (f32[7,2,128,128]{3,2,1,0:T(8,128)S(1)}, f32[7,2,128,128]{3,2,1,0:T(8,128)}, u32[]{:S(2)}) copy-start(f32[7,2,128,128]{3,2,1,0:T(8,128)} %fusion.87) | copy-start | bytes 2752516
  224.5 5.5 %copy-start.6 = (f32[7,2,128,128]{3,2,1,0:T(8,128)S(1)}, f32[7,2,128,128]{3,2,1,0:T(8,128)}, u32[]{:S(2)}) copy-start(f32[7,2,128,128]{3,2,1,0:T(8,128)} %fusion.90) | copy-start | bytes 2752516
  225.4 4.5 %copy-start.2 = (f32[7,2,128,128]{3,2,1,0:T(8,128)S(1)}, f32[7,2,128,128]{3,2,1,0:T(8,128)}, u32[]{:S(2)}) copy-start(f32[7,2,128,128]{3,2,1,0:T(8,128)} %fusion.94) | copy-start | bytes 2752516
  225.4 4.5 %copy-start.4 = (f32[7,2,128,128]{3,2,1,0:T(8,128)S(1)}, f32[7,2,128,128]{3,2,1,0:T(8,128)}, u32[]{:S(2)}) copy-start(f32[7,2,128,128]{3,2,1,0:T(8,128)} %fusion.92) | copy-start | bytes 2752516
  225.5 4.5 %copy-start.5 = (f32[7,2,128,128]{3,2,1,0:T(8,128)S(1)}, f32[7,2,128,128]{3,2,1,0:T(8,128)}, u32[]{:S(2)}) copy-start(f32[7,2,128,128]{3,2,1,0:T(8,128)} %fusion.91) | copy-start | bytes 2752516
  226.6 3.4 %copy-start.3 = (f32[7,2,128,128]{3,2,1,0:T(8,128)S(1)}, f32[7,2,128,128]{3,2,1,0:T(8,128)}, u32[]{:S(2)}) copy-start(f32[7,2,128,128]{3,2,1,0:T(8,128)} %fusion.93) | copy-start | bytes 2752516
  227.6 2.4 copy-start
  227.6 2.4 copy-start.1
  (3 other events, 2.3 us)
where the time goes:
time: 243 us; the launch traced here: 241 us
  matrix products  113 us (47%)
  waiting for transfers between devices  43.4 us (18%)
  starting transfers between devices  29.2 us (12%)
  other arithmetic  28.5 us (12%)
  local copies, waits for them, and re-layouts  25.5 us (10%)
    dot_general x84, matrix products, band_times(): jnp.einsum('qxy,bqyz->bqxz', term_band[shift_by + BAND], slab[low_b + BAN...  113 us
    ppermute x12, waiting for transfers between devices, shifted(): lax.ppermute(array, axis, [(i, (i + by) % peers) for i in range(peers)])  43.4 us
    ppermute x12, starting transfers between devices, shifted(): lax.ppermute(array, axis, [(i, (i + by) % peers) for i in range(peers)])  29.2 us
    scatter-add x24, local copies, waits for them, and re-layouts, band_times(): accum.at[low_b + shift_by + BAND:high_b + shift_by + BAND + 1]  19.9 us
    convert_element_type x11, other arithmetic, body(): newer = following.astype(jnp.bfloat16)  13.1 us
    unnamed x2, other arithmetic  13 us
  transfers between devices with their start and end apart: 12, of which 5 were waited for; matrix products, arithmetic and copies ran while one was open for 2% of the time, Pallas kernels for 0%

commit v1 on v0

v1 whole, which is shorter than its diff:
```python
import functools

import jax
import jax.numpy as jnp
from jax import lax
from jax.experimental import pallas as pl
from jax.experimental.pallas import tpu as pltpu
from jax.sharding import PartitionSpec as P

BAND = 3
TERMS = 12
GROUPS = ((0, 2), (2, 4), (4, 6), (6, 7))


def towards_lower(rows, cols, slot):
    pairs = []
    for r in range(rows):
        for c in range(cols):
            if c > 0:
                dst = r * cols + c - 1
            else:
                dst = ((r - 1 + slot) % rows) * cols + cols - 1
            pairs.append((r * cols + c, dst))
    return pairs


def towards_upper(rows, cols, slot):
    pairs = []
    for r in range(rows):
        for c in range(cols):
            if c < cols - 1:
                dst = r * cols + c + 1
            else:
                dst = ((r + slot) % rows) * cols
            pairs.append((r * cols + c, dst))
    return pairs


def terms_kernel(weights, scale, swaps, own, prev, now, *refs):
    rows, block = 2, own.shape[-1]
    offsets = own.shape[0]
    after = refs[: BAND * rows]
    before = refs[BAND * rows : 2 * BAND * rows]
    density, out_before, out_last, table, older, newer, total, sems = refs[2 * BAND * rows :]

    def cols(o):
        return slice(o * block, (o + 1) * block)

    for row in range(rows):
        table[row, cols(4), cols(0)] = jnp.zeros((block, block), jnp.bfloat16)
        table[row, cols(6), cols(2)] = jnp.zeros((block, block), jnp.bfloat16)
        table[row, cols(1), cols(5)] = jnp.zeros((block, block), jnp.bfloat16)
        for o in range(offsets):
            table[row, cols(BAND), cols(o)] = own[o, row]
        for dist in range(1, BAND + 1):
            for side in range(2):
                slabs = (after, before)[side]
                swapped = swaps[side * BAND + dist - 1] > 0
                for flip in range(2):
                    slab = slabs[(dist - 1) * rows + (row ^ flip)]

                    @pl.when(swapped if flip else jnp.logical_not(swapped))
                    def _():
                        for k in range(offsets - dist):
                            if side == 0:
                                table[row, cols(BAND + dist), cols(dist + k)] = slab[k]
                            else:
                                table[row, cols(BAND - dist), cols(offsets - 1 - dist - k)] = slab[k]

        for o in range(offsets):
            live = scale[row, o] > 0.0
            older[row, :, cols(o)] = jnp.where(live, prev[o, row], jnp.zeros((), jnp.bfloat16))
            newer[row, :, cols(o)] = jnp.where(live, now[o, row], jnp.zeros((), jnp.bfloat16))

    def term(step, cur, oth, first, last):
        weight = weights[step]
        for row in range(rows):
            for low, high in GROUPS:
                start, stop = max(0, low - BAND), min(offsets, high + BAND)
                product = jnp.dot(
                    cur[row, :, start * block : stop * block],
                    table[row, start * block : stop * block, low * block : high * block],
                    preferred_element_type=jnp.float32,
                )
                for o in range(low, high):
                    part = product[:, (o - low) * block : (o - low + 1) * block]
                    following = scale[row, o] * part - oth[row, :, cols(o)].astype(jnp.float32)
                    if first:
                        total[o, row] = weight * following
                    else:
                        total[o, row] += weight * following
                    oth[row, :, cols(o)] = following.astype(jnp.bfloat16)
                    if last:
                        copy_out(0, o, row).start()
                        copy_out(2, o, row).start()

    def copy_out(which, o, row):
        if which == 0:
            return pltpu.make_async_copy(total.at[o, row], density.at[o, row], sems.at[0, row, o])
        src = older if which == 1 else newer
        dst = out_before if which == 1 else out_last
        return pltpu.make_async_copy(src.at[row, :, cols(o)], dst.at[o, row], sems.at[which, row, o])

    term(0, newer, older, True, False)

    def pair(i, carry):
        term(2 * i + 1, older, newer, False, False)
        term(2 * i + 2, newer, older, False, False)
        return carry

    lax.fori_loop(0, (TERMS - 2) // 2, pair, 0)
    for row in range(rows):
        for o in range(offsets):
            copy_out(1, o, row).start()
    term(TERMS - 1, older, newer, False, True)
    for which in range(3):
        for row in range(rows):
            for o in range(offsets):
                copy_out(which, o, row).wait()


def body(hamiltonian, term_prev, term_now, pattern, weights):
    out_shape = hamiltonian.shape
    offsets, rows, block = out_shape[0], out_shape[1], out_shape[3]
    band_shape = (offsets, rows, block, block)
    row_count, col_count = lax.axis_size("row"), lax.axis_size("col")
    col = lax.axis_index("col")
    live = pattern.reshape(offsets, rows)
    own = hamiltonian.reshape(band_shape) * live.astype(jnp.bfloat16)[:, :, None, None]
    lower = [towards_lower(row_count, col_count, slot) for slot in range(rows)]
    upper = [towards_upper(row_count, col_count, slot) for slot in range(rows)]
    down = [own[: offsets - 1, slot] for slot in range(rows)]
    up = [own[:0:-1, slot] for slot in range(rows)]
    after, before = [], []
    for dist in range(1, BAND + 1):
        for slot in range(rows):
            down[slot] = lax.ppermute(down[slot][: offsets - dist], ("row", "col"), lower[slot])
            up[slot] = lax.ppermute(up[slot][: offsets - dist], ("row", "col"), upper[slot])
        after += down
        before += up
    swaps = jnp.stack(
        [col + dist >= col_count for dist in range(1, BAND + 1)]
        + [col < dist for dist in range(1, BAND + 1)]
    ).astype(jnp.int32)
    scale = 2.0 * live.T.astype(jnp.float32)

    vmem = pl.BlockSpec(memory_space=pltpu.VMEM)
    smem = pl.BlockSpec(memory_space=pltpu.SMEM)
    hbm = pl.BlockSpec(memory_space=pl.ANY)
    density, last_but_one, last = pl.pallas_call(
        terms_kernel,
        out_shape=(
            jax.ShapeDtypeStruct(band_shape, jnp.float32),
            jax.ShapeDtypeStruct(band_shape, jnp.bfloat16),
            jax.ShapeDtypeStruct(band_shape, jnp.bfloat16),
        ),
        in_specs=[smem] * 3 + [vmem] * (3 + len(after) + len(before)),
        out_specs=(hbm, hbm, hbm),
        scratch_shapes=[
            pltpu.VMEM((rows, offsets * block, offsets * block), jnp.bfloat16),
            pltpu.VMEM((rows, block, offsets * block), jnp.bfloat16),
            pltpu.VMEM((rows, block, offsets * block), jnp.bfloat16),
            pltpu.VMEM(band_shape, jnp.float32),
            pltpu.SemaphoreType.DMA((3, rows, offsets)),
        ],
        compiler_params=pltpu.CompilerParams(vmem_limit_bytes=32 * 2**20),
        cost_estimate=pl.CostEstimate(
            flops=2 * TERMS * rows * 37 * block**3, bytes_accessed=6 * 2**20, transcendentals=0
        ),
    )(
        weights,
        scale,
        swaps,
        own,
        term_prev.reshape(band_shape),
        term_now.reshape(band_shape),
        *after,
        *before,
    )
    return density.reshape(out_shape), last_but_one.reshape(out_shape), last.reshape(out_shape)


def solution(mesh):
    placed = P(None, "row", "col", None, None)
    return jax.shard_map(
        body,
        mesh=mesh,
        in_specs=(placed, placed, placed, P(None, "row", "col"), P()),
        out_specs=(placed, placed, placed),
        check_vma=False,
    )
```

time: 243 us -> 52.6 us (0.22)
  matrix products: 113 us -> 0 us
  waiting for transfers between devices: 43.4 us -> 12.5 us
  other arithmetic: 28.5 us -> 1.81 us
  local copies, waits for them, and re-layouts: 25.5 us -> 1.07 us
  Pallas kernels: 0 us -> 8.75 us
  starting transfers between devices: 29.2 us -> 26.7 us
    dot_general x84 -> x0, matrix products: 113 us -> none  [band_times(): jnp.einsum('qxy,bqyz->bqxz', term_band[shift_by + BAND], slab[low_b + BAN...]
    ppermute x12, waiting for transfers between devices: 43.4 us -> 12.5 us  [the longest x6 11.5 us: body(): lax.ppermute(up[slot][:offsets - dist], ('row', 'col'), upper[slot])]
    scatter-add x24 -> x0, local copies, waits for them, and re-layouts: 19.9 us -> none  [band_times(): accum.at[low_b + shift_by + BAND:high_b + shift_by + BAND + 1]]
    convert_element_type x13 -> x2, other arithmetic: 15.2 us -> 0.69 us  [the longest x1 0.68 us: body(): live.astype(jnp.bfloat16)[:, :, None, None]]
    unnamed x2 -> x0, other arithmetic: 13 us -> none
    pallas_call x0 -> x1, Pallas kernels: none -> 8.75 us  [body(): pl.pallas_call(terms_kernel, out_shape=(jax.ShapeDtypeStruct(band_shape,...]
    unnamed x46 -> x9, local copies, waits for them, and re-layouts: 4.66 us -> 0.67 us
    ppermute x12, starting transfers between devices: 29.2 us -> 26.7 us  [the longest x6 20.7 us: body(): lax.ppermute(down[slot][:offsets - dist], ('row', 'col'), lower[slot])]
  transfers between devices with their start and end apart: 12 -> 12, of which waited for: 5 -> 5; matrix products, arithmetic and copies ran while one was open for 2% -> 0% of each run, Pallas kernels for 0% -> 0%
where the time goes in v1:
time: 52.6 us; the launch traced here: 51.6 us
  starting transfers between devices  26.7 us (51%)
  waiting for transfers between devices  12.5 us (24%)
  Pallas kernels  8.75 us (17%)
  other arithmetic  1.81 us (3%)
  local copies, waits for them, and re-layouts  1.07 us (2%)
  between operations  0.79 us (2%)
    ppermute x6, starting transfers between devices, body(): lax.ppermute(down[slot][:offsets - dist], ('row', 'col'), lower[slot])  20.7 us
    ppermute x6, waiting for transfers between devices, body(): lax.ppermute(up[slot][:offsets - dist], ('row', 'col'), upper[slot])  11.5 us
    pallas_call x1, Pallas kernels, body(): pl.pallas_call(terms_kernel, out_shape=(jax.ShapeDtypeStruct(band_shape,...  8.75 us
    ppermute x6, starting transfers between devices, body(): lax.ppermute(up[slot][:offsets - dist], ('row', 'col'), upper[slot])  6 us
    mul x1, other arithmetic, body(): hamiltonian.reshape(band_shape)  1.11 us
  transfers between devices with their start and end apart: 12, of which 5 were waited for; matrix products, arithmetic and copies ran while one was open for 0% of the time, Pallas kernels for 0%

profile of v1, /device:TPU:1, one launch (start us, length us, event | category | flops | bytes accessed | tf_op | source)
XLA Modules:
  0.0 51.6 jit_solution(2601868893755879501)
XLA Ops:
  0.6 0.7 %convert_element_type.20 = bf16[7,2,1]{0,2,1:T(2,128)(2,1)S(1)} convert(s32[7,2,1]{0,2,1:T(1,128)} %param.8) | non-fusion elementwise | flops 14 | bytes 84 | tf_op jit(solution)/shard_map/convert_element_type | solution.py:129
  1.3 1.1 %bitcast_multiply_fusion = bf16[7,2,128,128]{3,2,0,1:T(8,128)(2,1)S(1)} fusion(bf16[7,2,1,128,128]{4,3,2,1,0:T(8,128)(2,1)} %param.5, bf16[7,2]{0,1:T(2,128)(2,1)S(1)} %bitcast.36), kind=kLoop, calls=%fused_computation | loop fusion | flops 229376 | bytes 917532 | tf_op jit(solution)/shard_map/mul | solution.py:129
  2.4 0.2 fusion
  2.6 2.5 %collective-permute-start.6 = (bf16[6,128,128]{2,1,0:T(8,128)(2,1)S(1)}, bf16[6,128,128]{2,1,0:T(8,128)(2,1)S(1)}, u32[]{:S(2)}, u32[]{:S(2)}) collective-permute-start(bf16[6,128,128]{2,1,0:T(8,128)(2,1)S(1)} %reverse_bitcast_fusion.1), channel_id=1, source_target_pairs={{0,1},{1,2},{2,3},{3,4},{4,5},{5,6},{6,7},{7,8},{8,9},{9,10},{10,1... | collective-permute-start | bytes 589832 | tf_op jit(solution)/shard_map/ppermute | solution.py:138
  5.2 1.7 %collective-permute-start.7 = (bf16[6,128,128]{2,1,0:T(8,128)(2,1)S(1)}, bf16[6,128,128]{2,1,0:T(8,128)(2,1)S(1)}, u32[]{:S(2)}, u32[]{:S(2)}) collective-permute-start(bf16[6,128,128]{2,1,0:T(8,128)(2,1)S(1)} %reverse_bitcast_fusion), channel_id=1, source_target_pairs={{0,1},{1,2},{2,3},{3,4},{4,5},{5,6},{6,7},{7,8},{8,9},{9,10},{10,1... | collective-permute-start | bytes 589832 | tf_op jit(solution)/shard_map/ppermute | solution.py:138
  6.9 4.9 %collective-permute-start.1 = (bf16[6,128,128]{2,1,0:T(8,128)(2,1)S(1)}, bf16[6,128,128]{2,1,0:T(8,128)(2,1)S(1)}, u32[]{:S(2)}, u32[]{:S(2)}) collective-permute-start(bf16[6,128,128]{2,1,0:T(8,128)(2,1)S(1)} %get-tuple-element.14), channel_id=1, source_target_pairs={{0,31},{1,0},{2,1},{3,2},{4,3},{5,4},{6,5},{7,6},{8,7},{9,8},{10,9... | collective-permute-start | bytes 589832 | tf_op jit(solution)/shard_map/ppermute | solution.py:137
  11.8 2.5 %collective-permute-start = (bf16[6,128,128]{2,1,0:T(8,128)(2,1)S(1)}, bf16[6,128,128]{2,1,0:T(8,128)(2,1)S(1)}, u32[]{:S(2)}, u32[]{:S(2)}) collective-permute-start(bf16[6,128,128]{2,1,0:T(8,128)(2,1)S(1)} %get-tuple-element.15), channel_id=1, source_target_pairs={{0,255},{1,0},{2,1},{3,2},{4,3},{5,4},{6,5},{7,6},{8,7},{9,8},{10,... | collective-permute-start | bytes 589832 | tf_op jit(solution)/shard_map/ppermute | solution.py:137
  14.3 1.9 %collective-permute-done.6.refs_6_ = bf16[6,128,128]{2,1,0:T(8,128)(2,1)S(1)} collective-permute-done((bf16[6,128,128]{2,1,0:T(8,128)(2,1)S(1)}, bf16[6,128,128]{2,1,0:T(8,128)(2,1)S(1)}, u32[]{:S(2)}, u32[]{:S(2)}) %collective-permute-start.6) | collective-permute-done | bytes 196640 | tf_op jit(solution)/shard_map/ppermute | solution.py:138
  16.2 0.1 collective-permute-start.8
  16.3 5.1 %collective-permute-done.7.refs_7_ = bf16[6,128,128]{2,1,0:T(8,128)(2,1)S(1)} collective-permute-done((bf16[6,128,128]{2,1,0:T(8,128)(2,1)S(1)}, bf16[6,128,128]{2,1,0:T(8,128)(2,1)S(1)}, u32[]{:S(2)}, u32[]{:S(2)}) %collective-permute-start.7) | collective-permute-done | bytes 196640 | tf_op jit(solution)/shard_map/ppermute | solution.py:138
  21.4 0.1 collective-permute-start.9
  21.5 0.0 collective-permute-done.1.refs_1_
  21.5 5.1 %collective-permute-start.3 = (bf16[5,128,128]{2,1,0:T(8,128)(2,1)S(1)}, bf16[5,128,128]{2,1,0:T(8,128)(2,1)S(1)}, u32[]{:S(2)}, u32[]{:S(2)}) collective-permute-start(bf16[5,128,128]{2,1,0:T(8,128)(2,1)S(1)} %slice.51), channel_id=1, source_target_pairs={{0,31},{1,0},{2,1},{3,2},{4,3},{5,4},{6,5},{7,6},{8,7},{9,8},{10,9... | collective-permute-start | bytes 491528 | tf_op jit(solution)/shard_map/ppermute | solution.py:137
  26.6 0.0 collective-permute-done.refs_0_
  26.6 0.1 collective-permute-start.2
  26.8 0.1 stack.27
  26.9 0.0 collective-permute-done.8.refs_8_
  26.9 0.0 copy-start
  26.9 1.5 %collective-permute-start.10 = (bf16[4,128,128]{2,1,0:T(8,128)(2,1)S(1)}, bf16[4,128,128]{2,1,0:T(8,128)(2,1)S(1)}, u32[]{:S(2)}, u32[]{:S(2)}) collective-permute-start(bf16[4,128,128]{2,1,0:T(8,128)(2,1)S(1)} %slice.58), channel_id=1, source_target_pairs={{0,1},{1,2},{2,3},{3,4},{4,5},{5,6},{6,7},{7,8},{8,9},{9,10},{10,1... | collective-permute-start | bytes 393224 | tf_op jit(solution)/shard_map/ppermute | solution.py:138
  28.4 2.5 %collective-permute-done.9.refs_9_ = bf16[5,128,128]{2,1,0:T(8,128)(2,1)S(1)} collective-permute-done((bf16[5,128,128]{2,1,0:T(8,128)(2,1)S(1)}, bf16[5,128,128]{2,1,0:T(8,128)(2,1)S(1)}, u32[]{:S(2)}, u32[]{:S(2)}) %collective-permute-start.9) | collective-permute-done | bytes 163872 | tf_op jit(solution)/shard_map/ppermute | solution.py:138
  30.9 0.1 collective-permute-start.11
  31.0 0.0 collective-permute-done.3.refs_3_
  31.1 0.0 copy-start.3
  31.1 6.2 %collective-permute-start.5 = (bf16[4,128,128]{2,1,0:T(8,128)(2,1)S(1)}, bf16[4,128,128]{2,1,0:T(8,128)(2,1)S(1)}, u32[]{:S(2)}, u32[]{:S(2)}) collective-permute-start(bf16[4,128,128]{2,1,0:T(8,128)(2,1)S(1)} %slice.53), channel_id=1, source_target_pairs={{0,31},{1,0},{2,1},{3,2},{4,3},{5,4},{6,5},{7,6},{8,7},{9,8},{10,9... | collective-permute-start | bytes 393224 | tf_op jit(solution)/shard_map/ppermute | solution.py:137
  37.2 0.0 collective-permute-done.2.refs_2_
  37.3 1.9 %collective-permute-start.4 = (bf16[4,128,128]{2,1,0:T(8,128)(2,1)S(1)}, bf16[4,128,128]{2,1,0:T(8,128)(2,1)S(1)}, u32[]{:S(2)}, u32[]{:S(2)}) collective-permute-start(bf16[4,128,128]{2,1,0:T(8,128)(2,1)S(1)} %slice.52), channel_id=1, source_target_pairs={{0,255},{1,0},{2,1},{3,2},{4,3},{5,4},{6,5},{7,6},{8,7},{9,8},{10,... | collective-permute-start | bytes 393224 | tf_op jit(solution)/shard_map/ppermute | solution.py:137
  39.2 0.0 collective-permute-done.10.refs_10_
  39.2 2.1 %collective-permute-done.11.refs_11_ = bf16[4,128,128]{2,1,0:T(8,128)(2,1)S(1)} collective-permute-done((bf16[4,128,128]{2,1,0:T(8,128)(2,1)S(1)}, bf16[4,128,128]{2,1,0:T(8,128)(2,1)S(1)}, u32[]{:S(2)}, u32[]{:S(2)}) %collective-permute-start.11) | collective-permute-done | bytes 131104 | tf_op jit(solution)/shard_map/ppermute | solution.py:138
  41.3 0.0 collective-permute-done.5.refs_5_
  41.3 0.9 %collective-permute-done.4.refs_4_ = bf16[4,128,128]{2,1,0:T(8,128)(2,1)S(1)} collective-permute-done((bf16[4,128,128]{2,1,0:T(8,128)(2,1)S(1)}, bf16[4,128,128]{2,1,0:T(8,128)(2,1)S(1)}, u32[]{:S(2)}, u32[]{:S(2)}) %collective-permute-start.4) | collective-permute-done | bytes 131104 | tf_op jit(solution)/shard_map/ppermute | solution.py:137
  42.2 0.6 %copy-done.2 = f32[12]{0:T(128)S(1)} copy-done((f32[12]{0:T(128)S(1)}, f32[12]{0:T(128)}, u32[]{:S(2)}) %copy-start.2) | copy-done | bytes 72
  42.9 8.8 %shard_map.76 = (f32[7,2,128,128]{3,2,1,0:T(8,128)}, bf16[7,2,128,128]{3,2,1,0:T(8,128)(2,1)}, bf16[7,2,128,128]{3,2,1,0:T(8,128)(2,1)}) custom-call(f32[12]{0:T(128)S(1)} %copy-done.2, f32[2,7]{1,0:T(2,128)S(1)} %bitcast.33, s32[6]{0:T(128)S(1)} %convert_element_type.19.swaps, bf16[7,2,128,128]{3,2,1,0:T(8,128)(2,1)S(1)} %copy.9.own, ...), custom_call_target="tpu_custom_call" | custom-call | flops 3724541952 | bytes 6291456 | tf_op jit(solution)/shard_map/pallas_call | solution.py:150
  (19 shorter events, 0.2 us)
Async XLA Ops:
  2.6 13.6 %collective-permute-start.6 = (bf16[6,128,128]{2,1,0:T(8,128)(2,1)S(1)}, bf16[6,128,128]{2,1,0:T(8,128)(2,1)S(1)}, u32[]{:S(2)}, u32[]{:S(2)}) collective-permute-start(bf16[6,128,128]{2,1,0:T(8,128)(2,1)S(1)} %reverse_bitcast_fusion.1), channel_id=1, source_target_pairs={{0,1},{1,2},{2,3},{3,4},{4,5},{5,6},{6,7},{7,8},{8,9},{9,10},{10,1... | collective-permute-start | bytes 589832 | tf_op jit(solution)/shard_map/ppermute | solution.py:138
  5.2 16.2 %collective-permute-start.7 = (bf16[6,128,128]{2,1,0:T(8,128)(2,1)S(1)}, bf16[6,128,128]{2,1,0:T(8,128)(2,1)S(1)}, u32[]{:S(2)}, u32[]{:S(2)}) collective-permute-start(bf16[6,128,128]{2,1,0:T(8,128)(2,1)S(1)} %reverse_bitcast_fusion), channel_id=1, source_target_pairs={{0,1},{1,2},{2,3},{3,4},{4,5},{5,6},{6,7},{7,8},{8,9},{9,10},{10,1... | collective-permute-start | bytes 589832 | tf_op jit(solution)/shard_map/ppermute | solution.py:138
  6.9 14.6 %collective-permute-start.1 = (bf16[6,128,128]{2,1,0:T(8,128)(2,1)S(1)}, bf16[6,128,128]{2,1,0:T(8,128)(2,1)S(1)}, u32[]{:S(2)}, u32[]{:S(2)}) collective-permute-start(bf16[6,128,128]{2,1,0:T(8,128)(2,1)S(1)} %get-tuple-element.14), channel_id=1, source_target_pairs={{0,31},{1,0},{2,1},{3,2},{4,3},{5,4},{6,5},{7,6},{8,7},{9,8},{10,9... | collective-permute-start | bytes 589832 | tf_op jit(solution)/shard_map/ppermute | solution.py:137
  11.8 14.7 %collective-permute-start = (bf16[6,128,128]{2,1,0:T(8,128)(2,1)S(1)}, bf16[6,128,128]{2,1,0:T(8,128)(2,1)S(1)}, u32[]{:S(2)}, u32[]{:S(2)}) collective-permute-start(bf16[6,128,128]{2,1,0:T(8,128)(2,1)S(1)} %get-tuple-element.15), channel_id=1, source_target_pairs={{0,255},{1,0},{2,1},{3,2},{4,3},{5,4},{6,5},{7,6},{8,7},{9,8},{10,... | collective-permute-start | bytes 589832 | tf_op jit(solution)/shard_map/ppermute | solution.py:137
  16.2 10.7 %collective-permute-start.8 = (bf16[5,128,128]{2,1,0:T(8,128)(2,1)S(1)}, bf16[5,128,128]{2,1,0:T(8,128)(2,1)S(1)}, u32[]{:S(2)}, u32[]{:S(2)}) collective-permute-start(bf16[5,128,128]{2,1,0:T(8,128)(2,1)S(1)} %slice.56), channel_id=1, source_target_pairs={{0,1},{1,2},{2,3},{3,4},{4,5},{5,6},{6,7},{7,8},{8,9},{9,10},{10,1... | collective-permute-start | bytes 491528 | tf_op jit(solution)/shard_map/ppermute | solution.py:138
  21.4 9.6 %collective-permute-start.9 = (bf16[5,128,128]{2,1,0:T(8,128)(2,1)S(1)}, bf16[5,128,128]{2,1,0:T(8,128)(2,1)S(1)}, u32[]{:S(2)}, u32[]{:S(2)}) collective-permute-start(bf16[5,128,128]{2,1,0:T(8,128)(2,1)S(1)} %slice.57), channel_id=1, source_target_pairs={{0,1},{1,2},{2,3},{3,4},{4,5},{5,6},{6,7},{7,8},{8,9},{9,10},{10,1... | collective-permute-start | bytes 491528 | tf_op jit(solution)/shard_map/ppermute | solution.py:138
  21.5 9.6 %collective-permute-start.3 = (bf16[5,128,128]{2,1,0:T(8,128)(2,1)S(1)}, bf16[5,128,128]{2,1,0:T(8,128)(2,1)S(1)}, u32[]{:S(2)}, u32[]{:S(2)}) collective-permute-start(bf16[5,128,128]{2,1,0:T(8,128)(2,1)S(1)} %slice.51), channel_id=1, source_target_pairs={{0,31},{1,0},{2,1},{3,2},{4,3},{5,4},{6,5},{7,6},{8,7},{9,8},{10,9... | collective-permute-start | bytes 491528 | tf_op jit(solution)/shard_map/ppermute | solution.py:137
  26.6 10.7 %collective-permute-start.2 = (bf16[5,128,128]{2,1,0:T(8,128)(2,1)S(1)}, bf16[5,128,128]{2,1,0:T(8,128)(2,1)S(1)}, u32[]{:S(2)}, u32[]{:S(2)}) collective-permute-start(bf16[5,128,128]{2,1,0:T(8,128)(2,1)S(1)} %slice.50), channel_id=1, source_target_pairs={{0,255},{1,0},{2,1},{3,2},{4,3},{5,4},{6,5},{7,6},{8,7},{9,8},{10,... | collective-permute-start | bytes 491528 | tf_op jit(solution)/shard_map/ppermute | solution.py:137
  26.9 15.3 %copy-start.1 = (bf16[7,2,1,128,128]{4,3,2,1,0:T(8,128)(2,1)S(1)}, bf16[7,2,1,128,128]{4,3,2,1,0:T(8,128)(2,1)}, u32[]{:S(2)}) copy-start(bf16[7,2,1,128,128]{4,3,2,1,0:T(8,128)(2,1)} %param.7) | copy-start | bytes 1376260
  26.9 15.3 %copy-start = (bf16[7,2,1,128,128]{4,3,2,1,0:T(8,128)(2,1)S(1)}, bf16[7,2,1,128,128]{4,3,2,1,0:T(8,128)(2,1)}, u32[]{:S(2)}) copy-start(bf16[7,2,1,128,128]{4,3,2,1,0:T(8,128)(2,1)} %param.6) | copy-start | bytes 1376260
  26.9 12.3 %collective-permute-start.10 = (bf16[4,128,128]{2,1,0:T(8,128)(2,1)S(1)}, bf16[4,128,128]{2,1,0:T(8,128)(2,1)S(1)}, u32[]{:S(2)}, u32[]{:S(2)}) collective-permute-start(bf16[4,128,128]{2,1,0:T(8,128)(2,1)S(1)} %slice.58), channel_id=1, source_target_pairs={{0,1},{1,2},{2,3},{3,4},{4,5},{5,6},{6,7},{7,8},{8,9},{9,10},{10,1... | collective-permute-start | bytes 393224 | tf_op jit(solution)/shard_map/ppermute | solution.py:138
  30.9 10.4 %collective-permute-start.11 = (bf16[4,128,128]{2,1,0:T(8,128)(2,1)S(1)}, bf16[4,128,128]{2,1,0:T(8,128)(2,1)S(1)}, u32[]{:S(2)}, u32[]{:S(2)}) collective-permute-start(bf16[4,128,128]{2,1,0:T(8,128)(2,1)S(1)} %slice.59), channel_id=1, source_target_pairs={{0,1},{1,2},{2,3},{3,4},{4,5},{5,6},{6,7},{7,8},{8,9},{9,10},{10,1... | collective-permute-start | bytes 393224 | tf_op jit(solution)/shard_map/ppermute | solution.py:138
  31.1 8.1 %copy-start.3 = (s32[7,2,1]{0,2,1:T(1,128)S(1)}, s32[7,2,1]{0,2,1:T(1,128)}, u32[]{:S(2)}) copy-start(s32[7,2,1]{0,2,1:T(1,128)} %param.8) | copy-start | bytes 172
  31.1 10.2 %collective-permute-start.5 = (bf16[4,128,128]{2,1,0:T(8,128)(2,1)S(1)}, bf16[4,128,128]{2,1,0:T(8,128)(2,1)S(1)}, u32[]{:S(2)}, u32[]{:S(2)}) collective-permute-start(bf16[4,128,128]{2,1,0:T(8,128)(2,1)S(1)} %slice.53), channel_id=1, source_target_pairs={{0,31},{1,0},{2,1},{3,2},{4,3},{5,4},{6,5},{7,6},{8,7},{9,8},{10,9... | collective-permute-start | bytes 393224 | tf_op jit(solution)/shard_map/ppermute | solution.py:137
  37.3 5.0 %collective-permute-start.4 = (bf16[4,128,128]{2,1,0:T(8,128)(2,1)S(1)}, bf16[4,128,128]{2,1,0:T(8,128)(2,1)S(1)}, u32[]{:S(2)}, u32[]{:S(2)}) collective-permute-start(bf16[4,128,128]{2,1,0:T(8,128)(2,1)S(1)} %slice.52), channel_id=1, source_target_pairs={{0,255},{1,0},{2,1},{3,2},{4,3},{5,4},{6,5},{7,6},{8,7},{9,8},{10,... | collective-permute-start | bytes 393224 | tf_op jit(solution)/shard_map/ppermute | solution.py:137
  42.2 0.7 %copy-start.2 = (f32[12]{0:T(128)S(1)}, f32[12]{0:T(128)}, u32[]{:S(2)}) copy-start(f32[12]{0:T(128)} %weights.1) | copy-start | bytes 148

commit v2 on v1

v2 whole, which is shorter than its diff:
```python
import functools

import jax
import jax.numpy as jnp
from jax import lax
from jax.experimental import pallas as pl
from jax.experimental.pallas import tpu as pltpu
from jax.sharding import PartitionSpec as P

BAND = 3
TERMS = 12
GROUPS = ((0, 2), (2, 4), (4, 6), (6, 7))


def even_first(rows, cols):
    return [(r * cols + c, r * cols + (c ^ 1)) for r in range(rows) for c in range(cols)]


def odd_first(rows, cols, slot):
    pairs = []
    for r in range(rows):
        for c in range(cols):
            if c % 2 == 1:
                dst = r * cols + c + 1 if c < cols - 1 else ((r + slot) % rows) * cols
            else:
                dst = r * cols + c - 1 if c > 0 else ((r - 1 + slot) % rows) * cols + cols - 1
            pairs.append((r * cols + c, dst))
    return pairs


def live_or_zero(live, block):
    return jnp.where(live, block, jnp.zeros((), block.dtype))


def mirror(offsets):
    odd = lax.rem(lax.axis_index("col"), 2)
    return lambda o: o + odd * (offsets - 1 - 2 * o)


def twice_or_zero(live, block):
    return live_or_zero(live, block + block)


def alive(pattern):
    offsets, rows = pattern.shape
    stored = mirror(offsets)
    return [[pattern[stored(o), row] > 0 for o in range(offsets)] for row in range(rows)]


def place(table, live, row, dist, side, slabs):
    offsets, block = 2 * BAND + 1, slabs[0].shape[-1]
    col, last = lax.axis_index("col"), lax.axis_size("col") - 1
    towards_last = lax.rem(col, 2) == side
    swapped = jnp.where(towards_last, last - col, col) < dist
    a = BAND + dist if side == 0 else BAND - dist
    for k in range(offsets - dist):
        o = dist + k if side == 0 else offsets - 1 - dist - k
        table[row, a * block : (a + 1) * block, o * block : (o + 1) * block] = twice_or_zero(
            live[row][o], jnp.where(swapped, slabs[1 - row][k], slabs[row][k])
        )


def start_kernel(pattern, weights, ham, prev, now, *refs):
    rows, offsets, block = 2, ham.shape[0], ham.shape[-1]
    near, far = refs[: (BAND - 1) * rows], refs[(BAND - 1) * rows : 2 * (BAND - 1) * rows]
    table, older, newer, tiles, got, scalars, sems = refs[2 * (BAND - 1) * rows :]
    stored = mirror(offsets)
    live = alive(pattern)

    def cols(o):
        return slice(o * block, (o + 1) * block)

    fetch = [pltpu.make_async_copy(src, got.at[i], sems.at[i]) for i, src in enumerate((ham, prev, now))]
    fetch.append(pltpu.make_async_copy(weights, scalars, sems.at[3]))
    for copy in fetch:
        copy.start()
    for row in range(rows):
        for a, o in ((4, 0), (1, 5)):
            table[row, cols(a), cols(o)] = jnp.zeros((block, block), jnp.bfloat16)
        for dist in range(1, BAND):
            for side, slabs in enumerate((near, far)):
                place(table, live, row, dist, side, slabs[(dist - 1) * rows : dist * rows])
    for copy in fetch:
        copy.wait()
    for row in range(rows):
        for o in range(offsets):
            at = stored(o)
            table[row, cols(BAND), cols(o)] = twice_or_zero(live[row][o], got[0, at, row])
            older[row, :, cols(o)] = live_or_zero(live[row][o], got[1, at, row])
            newer[row, :, cols(o)] = live_or_zero(live[row][o], got[2, at, row])
    for step in range(TERMS):
        tiles[step] = jnp.full(tiles.shape[1:], scalars[step])


def terms_kernel(pattern, near, near1, far, far1, tiles, table_in, older_in, newer_in, *refs):
    density, out_before, out_last, table, older, newer, total, out_sems = refs
    older[...] = older_in[...]
    newer[...] = newer_in[...]
    offsets, rows, block = total.shape[:3]
    stored = mirror(offsets)
    live = alive(pattern)

    def cols(o):
        return slice(o * block, (o + 1) * block)

    for row in range(rows):
        for a, start, stop in ((1, 0, 6), (2, 0, 6), (3, 0, 7), (4, 0, 7), (5, 2, 7)):
            part = (row, cols(a), slice(start * block, stop * block))
            table[part] = table_in[part]
        table[row, cols(6), cols(2)] = jnp.zeros((block, block), jnp.bfloat16)
        place(table, live, row, BAND, 0, (near, near1))
        place(table, live, row, BAND, 1, (far, far1))

    def copy_out(which, o, row):
        if which == 0:
            return pltpu.make_async_copy(total.at[o, row], density.at[stored(o), row], out_sems.at[0, row, o])
        src = older if which == 1 else newer
        dst = out_before if which == 1 else out_last
        return pltpu.make_async_copy(src.at[row, :, cols(o)], dst.at[stored(o), row], out_sems.at[which, row, o])

    for step in range(TERMS):
        cur, oth = (newer, older) if step % 2 == 0 else (older, newer)
        weight = tiles[step, :1]
        last = step == TERMS - 1
        for row in range(rows):
            for low, high in GROUPS:
                start, stop = max(0, low - BAND), min(offsets, high + BAND)
                product = jnp.dot(
                    cur[row, :, start * block : stop * block],
                    table[row, start * block : stop * block, low * block : high * block],
                    preferred_element_type=jnp.float32,
                )
                for o in range(low, high):
                    part = product[:, (o - low) * block : (o - low + 1) * block]
                    following = part - oth[row, :, cols(o)].astype(jnp.float32)
                    if step == 0:
                        total[o, row] = weight * following
                    else:
                        total[o, row] += weight * following
                    oth[row, :, cols(o)] = following.astype(jnp.bfloat16)
                    if last:
                        copy_out(0, o, row).start()
                        copy_out(2, o, row).start()
        if step == TERMS - 2:
            for row in range(rows):
                for o in range(offsets):
                    copy_out(1, o, row).start()
    for which in range(3):
        for row in range(rows):
            for o in range(offsets):
                copy_out(which, o, row).wait()


def body(hamiltonian, term_prev, term_now, pattern, weights):
    out_shape = hamiltonian.shape
    offsets, rows, block = out_shape[0], out_shape[1], out_shape[3]
    band_shape = (offsets, rows, block, block)
    row_count, col_count = lax.axis_size("row"), lax.axis_size("col")
    live = pattern.reshape(offsets, rows)
    vmem = pl.BlockSpec(memory_space=pltpu.VMEM)
    smem = pl.BlockSpec(memory_space=pltpu.SMEM)
    hbm = pl.BlockSpec(memory_space=pltpu.HBM)
    ham = hamiltonian.reshape(band_shape)
    kept = jnp.where(live[:, :, None, None] > 0, ham, jnp.zeros((), ham.dtype))
    odd = lax.axis_index("col") % 2 == 1
    low, high = kept[: offsets - 1], kept[:0:-1]
    pairs = even_first(row_count, col_count)
    across = [odd_first(row_count, col_count, slot) for slot in range(rows)]
    axes = ("row", "col")
    to_far = [jnp.where(odd, high[:, slot], low[:, slot]) for slot in range(rows)]
    to_near = [jnp.where(odd, low[:, slot], high[:, slot]) for slot in range(rows)]
    near, far = [], []
    for dist in range(1, BAND + 1):
        from_far, from_near = [], []
        for slot in range(rows):
            from_far.append(lax.ppermute(to_far[slot][: offsets - dist], axes, across[slot]))
            from_near.append(lax.ppermute(to_near[slot][: offsets - dist], axes, pairs))
        near += from_near
        far += from_far
        to_far, to_near = from_near, from_far

    table = jax.ShapeDtypeStruct((rows, offsets * block, offsets * block), jnp.bfloat16)
    term = jax.ShapeDtypeStruct((rows, block, offsets * block), jnp.bfloat16)
    held = (BAND - 1) * rows
    *begun, tiles = pl.pallas_call(
        start_kernel,
        out_shape=(table, term, term, jax.ShapeDtypeStruct((TERMS, 8, block), jnp.float32)),
        in_specs=[smem] + [hbm] * 4 + [vmem] * (2 * held),
        out_specs=(vmem,) * 4,
        scratch_shapes=[
            pltpu.VMEM((3, *band_shape), jnp.bfloat16),
            pltpu.SMEM((TERMS,), jnp.float32),
            pltpu.SemaphoreType.DMA((4,)),
        ],
        compiler_params=pltpu.CompilerParams(vmem_limit_bytes=10 * 2**20),
        cost_estimate=pl.CostEstimate(flops=0, bytes_accessed=4 * 2**20, transcendentals=0),
    )(
        live,
        weights,
        ham,
        term_prev.reshape(band_shape),
        term_now.reshape(band_shape),
        *near[:held],
        *far[:held],
    )
    density, last_but_one, last, *_ = pl.pallas_call(
        terms_kernel,
        out_shape=(
            jax.ShapeDtypeStruct(band_shape, jnp.float32),
            jax.ShapeDtypeStruct(band_shape, jnp.bfloat16),
            jax.ShapeDtypeStruct(band_shape, jnp.bfloat16),
        ),
        in_specs=[smem] + [vmem] * 8,
        out_specs=(hbm, hbm, hbm),
        scratch_shapes=[
            pltpu.VMEM(table.shape, table.dtype),
            pltpu.VMEM(term.shape, term.dtype),
            pltpu.VMEM(term.shape, term.dtype),
            pltpu.VMEM(band_shape, jnp.float32),
            pltpu.SemaphoreType.DMA((3, rows, offsets)),
        ],
        compiler_params=pltpu.CompilerParams(vmem_limit_bytes=10 * 2**20),
        cost_estimate=pl.CostEstimate(
            flops=2 * TERMS * rows * 37 * block**3, bytes_accessed=6 * 2**20, transcendentals=0
        ),
    )(live, *near[held:], *far[held:], tiles, *begun)
    return density.reshape(out_shape), last_but_one.reshape(out_shape), last.reshape(out_shape)


def solution(mesh):
    placed = P(None, "row", "col", None, None)
    return jax.shard_map(
        body,
        mesh=mesh,
        in_specs=(placed, placed, placed, P(None, "row", "col"), P()),
        out_specs=(placed, placed, placed),
        check_vma=False,
    )
```

time: 52.6 us -> 47.5 us (0.903)
  waiting for transfers between devices: 12.5 us -> 6.75 us
  starting transfers between devices: 26.7 us -> 25.2 us
  local copies, waits for them, and re-layouts: 1.07 us -> 2.18 us
  Pallas kernels: 8.75 us -> 9.58 us
    ppermute x12, waiting for transfers between devices: 12.5 us -> 6.75 us  [the longest x6 6.17 us: body(): lax.ppermute(to_far[slot][:offsets - dist], axes, across[slot])]
    pallas_call x0 -> x1, Pallas kernels: none -> 2.33 us  [body(): pl.pallas_call(start_kernel, out_shape=(table, term, term, jax.ShapeDtype...]
    slice x9, local copies, waits for them, and re-layouts: 0.24 us -> 2.07 us  [the longest x4 1.35 us: body(): from_near.append(lax.ppermute(to_near[slot][:offsets - dist], axes, pairs))]
    ppermute x12, starting transfers between devices: 26.7 us -> 25.2 us  [the longest x6 25 us: body(): lax.ppermute(to_far[slot][:offsets - dist], axes, across[slot])]
    pallas_call x1, Pallas kernels: 8.75 us -> 7.25 us  [body(): pl.pallas_call(terms_kernel, out_shape=(jax.ShapeDtypeStruct(band_shape,...]
    select_n x0 -> x3, other arithmetic: none -> 1.3 us  [the longest x1 1.11 us: body(): kept = jnp.where(live[:, :, None, None] > 0, ham, jnp.zeros((), ham.dtype))]
    mul x2 -> x0, other arithmetic: 1.12 us -> none  [the longest x1 1.11 us: body(): hamiltonian.reshape(band_shape)]
    gt x0 -> x1, other arithmetic: none -> 0.78 us  [body(): kept = jnp.where(live[:, :, None, None] > 0, ham, jnp.zeros((), ham.dtype))]
  transfers between devices with their start and end apart: 12 -> 12, of which waited for: 5 -> 4; matrix products, arithmetic and copies ran while one was open for 0% -> 5% of each run, Pallas kernels for 0% -> 5%
where the time goes in v2:
time: 47.5 us; the launch traced here: 46.8 us
  starting transfers between devices  25.2 us (53%)
  Pallas kernels  9.58 us (20%)
  waiting for transfers between devices  6.75 us (14%)
  local copies, waits for them, and re-layouts  2.18 us (5%)
  other arithmetic  2.08 us (4%)
  between operations  0.97 us (2%)
    ppermute x6, starting transfers between devices, body(): lax.ppermute(to_far[slot][:offsets - dist], axes, across[slot])  25 us
    pallas_call x1, Pallas kernels, body(): pl.pallas_call(terms_kernel, out_shape=(jax.ShapeDtypeStruct(band_shape,...  7.25 us
    ppermute x6, waiting for transfers between devices, body(): lax.ppermute(to_far[slot][:offsets - dist], axes, across[slot])  6.17 us
    pallas_call x1, Pallas kernels, body(): pl.pallas_call(start_kernel, out_shape=(table, term, term, jax.ShapeDtype...  2.33 us
    slice x4, local copies, waits for them, and re-layouts, body(): from_near.append(lax.ppermute(to_near[slot][:offsets - dist], axes, pairs))  1.35 us
    select_n x1, other arithmetic, body(): kept = jnp.where(live[:, :, None, None] > 0, ham, jnp.zeros((), ham.dtype))  1.11 us
  transfers between devices with their start and end apart: 12, of which 4 were waited for; matrix products, arithmetic and copies ran while one was open for 5% of the time, Pallas kernels for 5%

profile of v2, /device:TPU:1, one launch (start us, length us, event | category | flops | bytes accessed | tf_op | source)
XLA Modules:
  0.0 46.8 jit_solution(10695004059704795623)
XLA Ops:
  0.6 0.0 copy-start
  0.7 0.8 %broadcast_compare_fusion = pred[7,2]{0,1:T(4,128)(4,1)S(1)} fusion(s32[7,2]{0,1:T(2,128)} %bitcast.26), kind=kLoop, calls=%fused_computation.5 | loop fusion | flops 14 | bytes 70 | tf_op jit(solution)/shard_map/gt | solution.py:164
  1.5 1.1 %bitcast_select_fusion = bf16[7,2,128,128]{3,2,0,1:T(8,128)(2,1)S(1)} fusion(bf16[7,2,1,128,128]{4,3,2,1,0:T(8,128)(2,1)} %param.5, pred[7,2]{0,1:T(4,128)(4,1)S(1)} %broadcast_compare_fusion), kind=kLoop, calls=%fused_computation | loop fusion | flops 229376 | bytes 917518 | tf_op jit(solution)/shard_map/jit(_where)/select_n | solution.py:164
  2.6 0.1 select_bitcast_fusion
  2.7 9.0 %collective-permute-start.9 = (bf16[6,128,128]{2,1,0:T(8,128)(2,1)S(1)}, bf16[6,128,128]{2,1,0:T(8,128)(2,1)S(1)}, u32[]{:S(2)}, u32[]{:S(2)}) collective-permute-start(bf16[6,128,128]{2,1,0:T(8,128)(2,1)S(1)} %get-tuple-element.20), channel_id=1, source_target_pairs={{0,31},{1,2},{2,1},{3,4},{4,3},{5,6},{6,5},{7,8},{8,7},{9,10},{10,... | collective-permute-start | bytes 589832 | tf_op jit(solution)/shard_map/ppermute | solution.py:176
  11.7 0.0 collective-permute-start.3
  11.7 0.1 select_bitcast_fusion.1
  11.8 2.7 %collective-permute-start.6 = (bf16[6,128,128]{2,1,0:T(8,128)(2,1)S(1)}, bf16[6,128,128]{2,1,0:T(8,128)(2,1)S(1)}, u32[]{:S(2)}, u32[]{:S(2)}) collective-permute-start(bf16[6,128,128]{2,1,0:T(8,128)(2,1)S(1)} %get-tuple-element.22), channel_id=1, source_target_pairs={{0,255},{1,2},{2,1},{3,4},{4,3},{5,6},{6,5},{7,8},{8,7},{9,10},{10... | collective-permute-start | bytes 589832 | tf_op jit(solution)/shard_map/ppermute | solution.py:176
  14.4 0.0 collective-permute-start
  14.4 3.2 %collective-permute-done.9.refs_5_ = bf16[6,128,128]{2,1,0:T(8,128)(2,1)S(1)} collective-permute-done((bf16[6,128,128]{2,1,0:T(8,128)(2,1)S(1)}, bf16[6,128,128]{2,1,0:T(8,128)(2,1)S(1)}, u32[]{:S(2)}, u32[]{:S(2)}) %collective-permute-start.9) | collective-permute-done | bytes 196640 | tf_op jit(solution)/shard_map/ppermute | solution.py:176
  17.7 0.1 collective-permute-start.10
  17.8 0.0 collective-permute-done.3.refs_1_
  17.8 3.2 %collective-permute-start.4 = (bf16[5,128,128]{2,1,0:T(8,128)(2,1)S(1)}, bf16[5,128,128]{2,1,0:T(8,128)(2,1)S(1)}, u32[]{:S(2)}, u32[]{:S(2)}) collective-permute-start(bf16[5,128,128]{2,1,0:T(8,128)(2,1)S(1)} %slice.72), channel_id=1, source_target_pairs={{0,31},{1,2},{2,1},{3,4},{4,3},{5,6},{6,5},{7,8},{8,7},{9,10},{10,... | collective-permute-start | bytes 491528 | tf_op jit(solution)/shard_map/ppermute | solution.py:176
  21.0 0.3 collective-permute-done.6.refs_4_
  21.3 0.1 collective-permute-start.7
  21.4 0.0 collective-permute-done.refs_0_
  21.5 4.4 %collective-permute-start.1 = (bf16[5,128,128]{2,1,0:T(8,128)(2,1)S(1)}, bf16[5,128,128]{2,1,0:T(8,128)(2,1)S(1)}, u32[]{:S(2)}, u32[]{:S(2)}) collective-permute-start(bf16[5,128,128]{2,1,0:T(8,128)(2,1)S(1)} %slice.68), channel_id=1, source_target_pairs={{0,255},{1,2},{2,1},{3,4},{4,3},{5,6},{6,5},{7,8},{8,7},{9,10},{10... | collective-permute-start | bytes 491528 | tf_op jit(solution)/shard_map/ppermute | solution.py:176
  25.8 0.0 collective-permute-done.10.refs_3_
  25.9 1.3 %collective-permute-start.11 = (bf16[4,128,128]{2,1,0:T(8,128)(2,1)S(1)}, bf16[4,128,128]{2,1,0:T(8,128)(2,1)S(1)}, u32[]{:S(2)}, u32[]{:S(2)}) collective-permute-start(bf16[4,128,128]{2,1,0:T(8,128)(2,1)S(1)} %slice.77), channel_id=1, source_target_pairs={{0,31},{1,2},{2,1},{3,4},{4,3},{5,6},{6,5},{7,8},{8,7},{9,10},{10,... | collective-permute-start | bytes 393224 | tf_op jit(solution)/shard_map/ppermute | solution.py:176
  27.2 0.7 %slice.73 = bf16[4,128,128]{2,1,0:T(8,128)(2,1)} slice(bf16[5,128,128]{2,1,0:T(8,128)(2,1)S(1)} %collective-permute-done.4.refs_7_), slice={[0:4], [0:128], [0:128]} | slice | bytes 262144 | tf_op jit(solution)/shard_map/slice | solution.py:177
  27.8 0.0 collective-permute-start.5
  27.8 0.6 %collective-permute-done.7.refs_2_ = bf16[5,128,128]{2,1,0:T(8,128)(2,1)S(1)} collective-permute-done((bf16[5,128,128]{2,1,0:T(8,128)(2,1)S(1)}, bf16[5,128,128]{2,1,0:T(8,128)(2,1)S(1)}, u32[]{:S(2)}, u32[]{:S(2)}) %collective-permute-start.7) | collective-permute-done | bytes 163872 | tf_op jit(solution)/shard_map/ppermute | solution.py:177
  28.4 0.7 %slice.75 = bf16[4,128,128]{2,1,0:T(8,128)(2,1)} slice(bf16[5,128,128]{2,1,0:T(8,128)(2,1)S(1)} %collective-permute-done.7.refs_2_), slice={[0:4], [0:128], [0:128]} | slice | bytes 262144 | tf_op jit(solution)/shard_map/slice | solution.py:176
  29.1 4.5 %collective-permute-start.8 = (bf16[4,128,128]{2,1,0:T(8,128)(2,1)}, bf16[4,128,128]{2,1,0:T(8,128)(2,1)S(1)}, u32[]{:S(2)}, u32[]{:S(2)}) collective-permute-start(bf16[4,128,128]{2,1,0:T(8,128)(2,1)} %slice.75), channel_id=1, source_target_pairs={{0,255},{1,2},{2,1},{3,4},{4,3},{5,6},{6,5},{7,8},{8,7},{9,10},{10... | collective-permute-start | bytes 393224 | tf_op jit(solution)/shard_map/ppermute | solution.py:176
  33.6 0.7 %slice.69 = bf16[4,128,128]{2,1,0:T(8,128)(2,1)} slice(bf16[5,128,128]{2,1,0:T(8,128)(2,1)S(1)} %collective-permute-done.1.refs_6_), slice={[0:4], [0:128], [0:128]} | slice | bytes 262144 | tf_op jit(solution)/shard_map/slice | solution.py:177
  34.3 0.0 collective-permute-start.2
  34.3 0.1 copy.11.pattern
  34.4 2.3 %shard_map.76 = (bf16[2,896,896]{2,1,0:T(8,128)(2,1)S(1)}, bf16[2,128,896]{2,1,0:T(8,128)(2,1)S(1)}, bf16[2,128,896]{2,1,0:T(8,128)(2,1)S(1)}, f32[12,8,128]{2,1,0:T(8,128)S(1)}) custom-call(s32[7,2]{1,0:T(8,128)S(1)} %copy.11.pattern, f32[12]{0:T(128)S(1)} %copy-done.3, bf16[7,2,128,128]{3,2,1,0:T(8,128)(2,1)S(1)} %bitcast.23, ...), custom_call_target="tpu_custom_call" | custom-call | bytes 4194304 | tf_op jit(solution)/shard_map/pallas_call | solution.py:185
  36.7 0.0 collective-permute-done.11.far1
  36.7 2.6 %collective-permute-done.8.far = bf16[4,128,128]{2,1,0:T(8,128)(2,1)S(1)} collective-permute-done((bf16[4,128,128]{2,1,0:T(8,128)(2,1)}, bf16[4,128,128]{2,1,0:T(8,128)(2,1)S(1)}, u32[]{:S(2)}, u32[]{:S(2)}) %collective-permute-start.8) | collective-permute-done | bytes 131104 | tf_op jit(solution)/shard_map/ppermute | solution.py:176
  39.3 0.0 collective-permute-done.2.near
  39.3 7.3 %shard_map.77 = (f32[7,2,128,128]{3,2,1,0:T(8,128)}, bf16[7,2,128,128]{3,2,1,0:T(8,128)(2,1)}, bf16[7,2,128,128]{3,2,1,0:T(8,128)(2,1)}) custom-call(s32[7,2]{1,0:T(8,128)S(1)} %copy.11.pattern, bf16[4,128,128]{2,1,0:T(8,128)(2,1)S(1)} %collective-permute-done.2.near, bf16[4,128,128]{2,1,0:T(8,128)(2,1)S(1)} %collective-permute-done.5.near1, ...), custom_call_target="tpu_custom_call" | custom-call | flops 3724541952 | bytes 6291456 | tf_op jit(solution)/shard_map/pallas_call | solution.py:206
  (18 shorter events, 0.1 us)
Async XLA Ops:
  0.6 33.6 %copy-start.4 = (s32[7,2,1]{0,2,1:T(1,128)S(1)}, s32[7,2,1]{0,2,1:T(1,128)}, u32[]{:S(2)}) copy-start(s32[7,2,1]{0,2,1:T(1,128)} %param.8) | copy-start | bytes 172
  0.6 33.7 %copy-start = (bf16[7,2,1,128,128]{4,3,2,1,0:T(8,128)(2,1)S(1)}, bf16[7,2,1,128,128]{4,3,2,1,0:T(8,128)(2,1)}, u32[]{:S(2)}) copy-start(bf16[7,2,1,128,128]{4,3,2,1,0:T(8,128)(2,1)} %param.5) | copy-start | bytes 1376260
  0.7 33.7 %copy-start.3 = (f32[12]{0:T(128)S(1)}, f32[12]{0:T(128)}, u32[]{:S(2)}) copy-start(f32[12]{0:T(128)} %weights.1) | copy-start | bytes 148
  0.7 33.7 %copy-start.2 = (bf16[7,2,1,128,128]{4,3,2,1,0:T(8,128)(2,1)S(1)}, bf16[7,2,1,128,128]{4,3,2,1,0:T(8,128)(2,1)}, u32[]{:S(2)}) copy-start(bf16[7,2,1,128,128]{4,3,2,1,0:T(8,128)(2,1)} %param.7) | copy-start | bytes 1376260
  0.7 33.7 %copy-start.1 = (bf16[7,2,1,128,128]{4,3,2,1,0:T(8,128)(2,1)S(1)}, bf16[7,2,1,128,128]{4,3,2,1,0:T(8,128)(2,1)}, u32[]{:S(2)}) copy-start(bf16[7,2,1,128,128]{4,3,2,1,0:T(8,128)(2,1)} %param.6) | copy-start | bytes 1376260
  2.7 14.9 %collective-permute-start.9 = (bf16[6,128,128]{2,1,0:T(8,128)(2,1)S(1)}, bf16[6,128,128]{2,1,0:T(8,128)(2,1)S(1)}, u32[]{:S(2)}, u32[]{:S(2)}) collective-permute-start(bf16[6,128,128]{2,1,0:T(8,128)(2,1)S(1)} %get-tuple-element.20), channel_id=1, source_target_pairs={{0,31},{1,2},{2,1},{3,4},{4,3},{5,6},{6,5},{7,8},{8,7},{9,10},{10,... | collective-permute-start | bytes 589832 | tf_op jit(solution)/shard_map/ppermute | solution.py:176
  11.7 6.1 %collective-permute-start.3 = (bf16[6,128,128]{2,1,0:T(8,128)(2,1)S(1)}, bf16[6,128,128]{2,1,0:T(8,128)(2,1)S(1)}, u32[]{:S(2)}, u32[]{:S(2)}) collective-permute-start(bf16[6,128,128]{2,1,0:T(8,128)(2,1)S(1)} %get-tuple-element.21), channel_id=1, source_target_pairs={{0,1},{1,0},{2,3},{3,2},{4,5},{5,4},{6,7},{7,6},{8,9},{9,8},{10,11... | collective-permute-start | bytes 589832 | tf_op jit(solution)/shard_map/ppermute | solution.py:177
  11.8 9.6 %collective-permute-start.6 = (bf16[6,128,128]{2,1,0:T(8,128)(2,1)S(1)}, bf16[6,128,128]{2,1,0:T(8,128)(2,1)S(1)}, u32[]{:S(2)}, u32[]{:S(2)}) collective-permute-start(bf16[6,128,128]{2,1,0:T(8,128)(2,1)S(1)} %get-tuple-element.22), channel_id=1, source_target_pairs={{0,255},{1,2},{2,1},{3,4},{4,3},{5,6},{6,5},{7,8},{8,7},{9,10},{10... | collective-permute-start | bytes 589832 | tf_op jit(solution)/shard_map/ppermute | solution.py:176
  14.4 7.0 %collective-permute-start = (bf16[6,128,128]{2,1,0:T(8,128)(2,1)S(1)}, bf16[6,128,128]{2,1,0:T(8,128)(2,1)S(1)}, u32[]{:S(2)}, u32[]{:S(2)}) collective-permute-start(bf16[6,128,128]{2,1,0:T(8,128)(2,1)S(1)} %get-tuple-element.23), channel_id=1, source_target_pairs={{0,1},{1,0},{2,3},{3,2},{4,5},{5,4},{6,7},{7,6},{8,9},{9,8},{10,11... | collective-permute-start | bytes 589832 | tf_op jit(solution)/shard_map/ppermute | solution.py:177
  17.7 8.1 %collective-permute-start.10 = (bf16[5,128,128]{2,1,0:T(8,128)(2,1)S(1)}, bf16[5,128,128]{2,1,0:T(8,128)(2,1)S(1)}, u32[]{:S(2)}, u32[]{:S(2)}) collective-permute-start(bf16[5,128,128]{2,1,0:T(8,128)(2,1)S(1)} %slice.76), channel_id=1, source_target_pairs={{0,1},{1,0},{2,3},{3,2},{4,5},{5,4},{6,7},{7,6},{8,9},{9,8},{10,11... | collective-permute-start | bytes 491528 | tf_op jit(solution)/shard_map/ppermute | solution.py:177
  17.8 9.3 %collective-permute-start.4 = (bf16[5,128,128]{2,1,0:T(8,128)(2,1)S(1)}, bf16[5,128,128]{2,1,0:T(8,128)(2,1)S(1)}, u32[]{:S(2)}, u32[]{:S(2)}) collective-permute-start(bf16[5,128,128]{2,1,0:T(8,128)(2,1)S(1)} %slice.72), channel_id=1, source_target_pairs={{0,31},{1,2},{2,1},{3,4},{4,3},{5,6},{6,5},{7,8},{8,7},{9,10},{10,... | collective-permute-start | bytes 491528 | tf_op jit(solution)/shard_map/ppermute | solution.py:176
  21.3 7.1 %collective-permute-start.7 = (bf16[5,128,128]{2,1,0:T(8,128)(2,1)S(1)}, bf16[5,128,128]{2,1,0:T(8,128)(2,1)S(1)}, u32[]{:S(2)}, u32[]{:S(2)}) collective-permute-start(bf16[5,128,128]{2,1,0:T(8,128)(2,1)S(1)} %slice.74), channel_id=1, source_target_pairs={{0,1},{1,0},{2,3},{3,2},{4,5},{5,4},{6,7},{7,6},{8,9},{9,8},{10,11... | collective-permute-start | bytes 491528 | tf_op jit(solution)/shard_map/ppermute | solution.py:177
  21.5 12.1 %collective-permute-start.1 = (bf16[5,128,128]{2,1,0:T(8,128)(2,1)S(1)}, bf16[5,128,128]{2,1,0:T(8,128)(2,1)S(1)}, u32[]{:S(2)}, u32[]{:S(2)}) collective-permute-start(bf16[5,128,128]{2,1,0:T(8,128)(2,1)S(1)} %slice.68), channel_id=1, source_target_pairs={{0,255},{1,2},{2,1},{3,4},{4,3},{5,6},{6,5},{7,8},{8,7},{9,10},{10... | collective-permute-start | bytes 491528 | tf_op jit(solution)/shard_map/ppermute | solution.py:176
  25.9 10.9 %collective-permute-start.11 = (bf16[4,128,128]{2,1,0:T(8,128)(2,1)S(1)}, bf16[4,128,128]{2,1,0:T(8,128)(2,1)S(1)}, u32[]{:S(2)}, u32[]{:S(2)}) collective-permute-start(bf16[4,128,128]{2,1,0:T(8,128)(2,1)S(1)} %slice.77), channel_id=1, source_target_pairs={{0,31},{1,2},{2,1},{3,4},{4,3},{5,6},{6,5},{7,8},{8,7},{9,10},{10,... | collective-permute-start | bytes 393224 | tf_op jit(solution)/shard_map/ppermute | solution.py:176
  27.8 8.9 %collective-permute-start.5 = (bf16[4,128,128]{2,1,0:T(8,128)(2,1)}, bf16[4,128,128]{2,1,0:T(8,128)(2,1)S(1)}, u32[]{:S(2)}, u32[]{:S(2)}) collective-permute-start(bf16[4,128,128]{2,1,0:T(8,128)(2,1)} %slice.73), channel_id=1, source_target_pairs={{0,1},{1,0},{2,3},{3,2},{4,5},{5,4},{6,7},{7,6},{8,9},{9,8},{10,11... | collective-permute-start | bytes 393224 | tf_op jit(solution)/shard_map/ppermute | solution.py:177
  29.1 10.3 %collective-permute-start.8 = (bf16[4,128,128]{2,1,0:T(8,128)(2,1)}, bf16[4,128,128]{2,1,0:T(8,128)(2,1)S(1)}, u32[]{:S(2)}, u32[]{:S(2)}) collective-permute-start(bf16[4,128,128]{2,1,0:T(8,128)(2,1)} %slice.75), channel_id=1, source_target_pairs={{0,255},{1,2},{2,1},{3,4},{4,3},{5,6},{6,5},{7,8},{8,7},{9,10},{10... | collective-permute-start | bytes 393224 | tf_op jit(solution)/shard_map/ppermute | solution.py:176
  34.3 5.1 %collective-permute-start.2 = (bf16[4,128,128]{2,1,0:T(8,128)(2,1)}, bf16[4,128,128]{2,1,0:T(8,128)(2,1)S(1)}, u32[]{:S(2)}, u32[]{:S(2)}) collective-permute-start(bf16[4,128,128]{2,1,0:T(8,128)(2,1)} %slice.69), channel_id=1, source_target_pairs={{0,1},{1,0},{2,3},{3,2},{4,5},{5,4},{6,7},{7,6},{8,9},{9,8},{10,11... | collective-permute-start | bytes 393224 | tf_op jit(solution)/shard_map/ppermute | solution.py:177

commit v3 on v2

--- a/solution.py
+++ b/solution.py
@@ -9,6 +9,7 @@
 
 BAND = 3
 TERMS = 12
+LEAST = 5
 GROUPS = ((0, 2), (2, 4), (4, 6), (6, 7))
 
 
@@ -63,31 +64,28 @@
 def start_kernel(pattern, weights, ham, prev, now, *refs):
     rows, offsets, block = 2, ham.shape[0], ham.shape[-1]
     near, far = refs[: (BAND - 1) * rows], refs[(BAND - 1) * rows : 2 * (BAND - 1) * rows]
-    table, older, newer, tiles, got, scalars, sems = refs[2 * (BAND - 1) * rows :]
+    table, older, newer, tiles, scalars, sem = refs[2 * (BAND - 1) * rows :]
     stored = mirror(offsets)
     live = alive(pattern)
 
     def cols(o):
         return slice(o * block, (o + 1) * block)
 
-    fetch = [pltpu.make_async_copy(src, got.at[i], sems.at[i]) for i, src in enumerate((ham, prev, now))]
-    fetch.append(pltpu.make_async_copy(weights, scalars, sems.at[3]))
-    for copy in fetch:
-        copy.start()
+    fetch = pltpu.make_async_copy(weights, scalars, sem)
+    fetch.start()
     for row in range(rows):
         for a, o in ((4, 0), (1, 5)):
             table[row, cols(a), cols(o)] = jnp.zeros((block, block), jnp.bfloat16)
         for dist in range(1, BAND):
             for side, slabs in enumerate((near, far)):
                 place(table, live, row, dist, side, slabs[(dist - 1) * rows : dist * rows])
-    for copy in fetch:
-        copy.wait()
     for row in range(rows):
         for o in range(offsets):
             at = stored(o)
-            table[row, cols(BAND), cols(o)] = twice_or_zero(live[row][o], got[0, at, row])
-            older[row, :, cols(o)] = live_or_zero(live[row][o], got[1, at, row])
-            newer[row, :, cols(o)] = live_or_zero(live[row][o], got[2, at, row])
+            table[row, cols(BAND), cols(o)] = twice_or_zero(live[row][o], ham[at, row])
+            older[row, :, cols(o)] = live_or_zero(live[row][o], prev[at, row])
+            newer[row, :, cols(o)] = live_or_zero(live[row][o], now[at, row])
+    fetch.wait()
     for step in range(TERMS):
         tiles[step] = jnp.full(tiles.shape[1:], scalars[step])
 
@@ -103,7 +101,7 @@
     def cols(o):
         return slice(o * block, (o + 1) * block)
 
-    for row in range(rows):
+    def fill(row):
         for a, start, stop in ((1, 0, 6), (2, 0, 6), (3, 0, 7), (4, 0, 7), (5, 2, 7)):
             part = (row, cols(a), slice(start * block, stop * block))
             table[part] = table_in[part]
@@ -118,33 +116,36 @@
         dst = out_before if which == 1 else out_last
         return pltpu.make_async_copy(src.at[row, :, cols(o)], dst.at[stored(o), row], out_sems.at[which, row, o])
 
-    for step in range(TERMS):
+    def term(row, step):
         cur, oth = (newer, older) if step % 2 == 0 else (older, newer)
         weight = tiles[step, :1]
-        last = step == TERMS - 1
+        for low, high in GROUPS:
+            start, stop = max(0, low - BAND), min(offsets, high + BAND)
+            product = jnp.dot(
+                cur[row, :, start * block : stop * block],
+                table[row, start * block : stop * block, low * block : high * block],
+                preferred_element_type=jnp.float32,
+            )
+            for o in range(low, high):
+                part = product[:, (o - low) * block : (o - low + 1) * block]
+                following = part - oth[row, :, cols(o)].astype(jnp.float32)
+                if step == 0:
+                    total[o, row] = weight * following
+                else:
+                    total[o, row] += weight * following
+                oth[row, :, cols(o)] = following.astype(jnp.bfloat16)
+                if step == TERMS - 1:
+                    copy_out(0, o, row).start()
+                    copy_out(2, o, row).start()
+        if step == TERMS - 2:
+            for o in range(offsets):
+                copy_out(1, o, row).start()
+
+    for step in range(TERMS):
         for row in range(rows):
-            for low, high in GROUPS:
-                start, stop = max(0, low - BAND), min(offsets, high + BAND)
-                product = jnp.dot(
-                    cur[row, :, start * block : stop * block],
-                    table[row, start * block : stop * block, low * block : high * block],
-                    preferred_element_type=jnp.float32,
-                )
-                for o in range(low, high):
-                    part = product[:, (o - low) * block : (o - low + 1) * block]
-                    following = part - oth[row, :, cols(o)].astype(jnp.float32)
-                    if step == 0:
-                        total[o, row] = weight * following
-                    else:
-                        total[o, row] += weight * following
-                    oth[row, :, cols(o)] = following.astype(jnp.bfloat16)
-                    if last:
-                        copy_out(0, o, row).start()
-                        copy_out(2, o, row).start()
-        if step == TERMS - 2:
-            for row in range(rows):
-                for o in range(offsets):
-                    copy_out(1, o, row).start()
+            if step == 0:
+                fill(row)
+            term(row, step)
     for which in range(3):
         for row in range(rows):
             for o in range(offsets):
@@ -161,7 +162,7 @@
     smem = pl.BlockSpec(memory_space=pltpu.SMEM)
     hbm = pl.BlockSpec(memory_space=pltpu.HBM)
     ham = hamiltonian.reshape(band_shape)
-    kept = jnp.where(live[:, :, None, None] > 0, ham, jnp.zeros((), ham.dtype))
+    kept = ham * live.astype(ham.dtype)[:, :, None, None]
     odd = lax.axis_index("col") % 2 == 1
     low, high = kept[: offsets - 1], kept[:0:-1]
     pairs = even_first(row_count, col_count)
@@ -173,8 +174,8 @@
     for dist in range(1, BAND + 1):
         from_far, from_near = [], []
         for slot in range(rows):
-            from_far.append(lax.ppermute(to_far[slot][: offsets - dist], axes, across[slot]))
-            from_near.append(lax.ppermute(to_near[slot][: offsets - dist], axes, pairs))
+            from_far.append(lax.ppermute(to_far[slot][: max(offsets - dist, LEAST)], axes, across[slot]))
+            from_near.append(lax.ppermute(to_near[slot][: max(offsets - dist, LEAST)], axes, pairs))
         near += from_near
         far += from_far
         to_far, to_near = from_near, from_far
@@ -185,12 +186,11 @@
     *begun, tiles = pl.pallas_call(
         start_kernel,
         out_shape=(table, term, term, jax.ShapeDtypeStruct((TERMS, 8, block), jnp.float32)),
-        in_specs=[smem] + [hbm] * 4 + [vmem] * (2 * held),
+        in_specs=[smem, hbm] + [vmem] * (3 + 2 * held),
         out_specs=(vmem,) * 4,
         scratch_shapes=[
-            pltpu.VMEM((3, *band_shape), jnp.bfloat16),
             pltpu.SMEM((TERMS,), jnp.float32),
-            pltpu.SemaphoreType.DMA((4,)),
+            pltpu.SemaphoreType.DMA,
         ],
         compiler_params=pltpu.CompilerParams(vmem_limit_bytes=10 * 2**20),
         cost_estimate=pl.CostEstimate(flops=0, bytes_accessed=4 * 2**20, transcendentals=0),

time: 47.5 us -> 47.7 us (level); the launches traced: 46.8 us -> 47.5 us
  waiting for transfers between devices: 6.75 us -> 11.2 us
  local copies, waits for them, and re-layouts: 2.18 us -> 0.18 us
  Pallas kernels: 9.58 us -> 8.6 us
  starting transfers between devices: 25.2 us -> 24.5 us
    ppermute x12, waiting for transfers between devices: 6.75 us -> 11.2 us  [the longest x6 9.95 us: body(): lax.ppermute(to_far[slot][:max(offsets - dist, LEAST)], axes, across[slot])]
    slice x8 -> x4, local copies, waits for them, and re-layouts: 2.05 us -> 0.05 us  [the longest x2 0.03 us: body(): to_far[slot][:max(offsets - dist, LEAST)]]
    select_n x1 -> x0, other arithmetic: 1.11 us -> none  [body(): kept = jnp.where(live[:, :, None, None] > 0, ham, jnp.zeros((), ham.dtype))]
    mul x0 -> x1, other arithmetic: none -> 1.11 us  [body(): kept = ham * live.astype(ham.dtype)[:, :, None, None]]
    pallas_call x1, Pallas kernels: 2.33 us -> 1.4 us  [body(): pl.pallas_call(start_kernel, out_shape=(table, term, term, jax.ShapeDtype...]
    gt x1 -> x0, other arithmetic: 0.78 us -> none  [body(): kept = jnp.where(live[:, :, None, None] > 0, ham, jnp.zeros((), ham.dtype))]
    convert_element_type x0 -> x1, other arithmetic: none -> 0.78 us  [body(): kept = ham * live.astype(ham.dtype)[:, :, None, None]]
    ppermute x12, starting transfers between devices: 25.2 us -> 24.5 us  [the longest x6 24.3 us: body(): lax.ppermute(to_far[slot][:max(offsets - dist, LEAST)], axes, across[slot])]
  transfers between devices with their start and end apart: 12 -> 12, of which waited for: 4 -> 5; matrix products, arithmetic and copies ran while one was open for 5% -> 0% of each run, Pallas kernels for 5% -> 3%
where the time goes in v3:
time: 47.7 us; the launch traced here: 47.5 us
  starting transfers between devices  24.5 us (51%)
  waiting for transfers between devices  11.2 us (23%)
  Pallas kernels  8.6 us (18%)
  other arithmetic  2.08 us (4%)
  between operations  0.96 us (2%)
    ppermute x6, starting transfers between devices, body(): lax.ppermute(to_far[slot][:max(offsets - dist, LEAST)], axes, across[slot])  24.3 us
    ppermute x6, waiting for transfers between devices, body(): lax.ppermute(to_far[slot][:max(offsets - dist, LEAST)], axes, across[slot])  9.95 us
    pallas_call x1, Pallas kernels, body(): pl.pallas_call(terms_kernel, out_shape=(jax.ShapeDtypeStruct(band_shape,...  7.19 us
    pallas_call x1, Pallas kernels, body(): pl.pallas_call(start_kernel, out_shape=(table, term, term, jax.ShapeDtype...  1.4 us
    ppermute x6, waiting for transfers between devices, body(): lax.ppermute(to_near[slot][:max(offsets - dist, LEAST)], axes, pairs)  1.27 us
    mul x1, other arithmetic, body(): kept = ham * live.astype(ham.dtype)[:, :, None, None]  1.11 us
  transfers between devices with their start and end apart: 12, of which 5 were waited for; matrix products, arithmetic and copies ran while one was open for 0% of the time, Pallas kernels for 3%

profile of v3, /device:TPU:1, one launch (start us, length us, event | category | flops | bytes accessed | tf_op | source)
XLA Modules:
  0.0 47.5 jit_solution(10444176312695204556)
XLA Ops:
  0.6 0.0 copy-start
  0.7 0.8 %convert_element_type.7 = bf16[7,2]{0,1:T(2,128)(2,1)S(1)} convert(s32[7,2]{0,1:T(2,128)} %bitcast.26) | non-fusion elementwise | flops 14 | bytes 84 | tf_op jit(solution)/shard_map/convert_element_type | solution.py:165
  1.5 1.1 %bitcast_multiply_fusion = bf16[7,2,128,128]{3,2,0,1:T(8,128)(2,1)S(1)} fusion(bf16[7,2,1,128,128]{4,3,2,1,0:T(8,128)(2,1)} %param.5, bf16[7,2]{0,1:T(2,128)(2,1)S(1)} %convert_element_type.7), kind=kLoop, calls=%fused_computation | loop fusion | flops 229376 | bytes 917532 | tf_op jit(solution)/shard_map/mul | solution.py:165
  2.6 0.1 select_bitcast_fusion
  2.7 9.0 %collective-permute-start.9 = (bf16[6,128,128]{2,1,0:T(8,128)(2,1)S(1)}, bf16[6,128,128]{2,1,0:T(8,128)(2,1)S(1)}, u32[]{:S(2)}, u32[]{:S(2)}) collective-permute-start(bf16[6,128,128]{2,1,0:T(8,128)(2,1)S(1)} %get-tuple-element.20), channel_id=1, source_target_pairs={{0,31},{1,2},{2,1},{3,4},{4,3},{5,6},{6,5},{7,8},{8,7},{9,10},{10,... | collective-permute-start | bytes 589832 | tf_op jit(solution)/shard_map/ppermute | solution.py:177
  11.7 0.0 collective-permute-start.3
  11.7 0.1 select_bitcast_fusion.1
  11.8 2.7 %collective-permute-start.6 = (bf16[6,128,128]{2,1,0:T(8,128)(2,1)S(1)}, bf16[6,128,128]{2,1,0:T(8,128)(2,1)S(1)}, u32[]{:S(2)}, u32[]{:S(2)}) collective-permute-start(bf16[6,128,128]{2,1,0:T(8,128)(2,1)S(1)} %get-tuple-element.22), channel_id=1, source_target_pairs={{0,255},{1,2},{2,1},{3,4},{4,3},{5,6},{6,5},{7,8},{8,7},{9,10},{10... | collective-permute-start | bytes 589832 | tf_op jit(solution)/shard_map/ppermute | solution.py:177
  14.4 0.0 collective-permute-start
  14.4 3.2 %collective-permute-done.9.refs_5_ = bf16[6,128,128]{2,1,0:T(8,128)(2,1)S(1)} collective-permute-done((bf16[6,128,128]{2,1,0:T(8,128)(2,1)S(1)}, bf16[6,128,128]{2,1,0:T(8,128)(2,1)S(1)}, u32[]{:S(2)}, u32[]{:S(2)}) %collective-permute-start.9) | collective-permute-done | bytes 196640 | tf_op jit(solution)/shard_map/ppermute | solution.py:177
  17.7 0.1 collective-permute-start.10
  17.8 0.0 collective-permute-done.3.refs_1_
  17.8 3.2 %collective-permute-start.4 = (bf16[5,128,128]{2,1,0:T(8,128)(2,1)S(1)}, bf16[5,128,128]{2,1,0:T(8,128)(2,1)S(1)}, u32[]{:S(2)}, u32[]{:S(2)}) collective-permute-start(bf16[5,128,128]{2,1,0:T(8,128)(2,1)S(1)} %slice.55), channel_id=1, source_target_pairs={{0,31},{1,2},{2,1},{3,4},{4,3},{5,6},{6,5},{7,8},{8,7},{9,10},{10,... | collective-permute-start | bytes 491528 | tf_op jit(solution)/shard_map/ppermute | solution.py:177
  21.0 0.3 collective-permute-done.6.refs_4_
  21.3 0.1 collective-permute-start.7
  21.4 0.0 collective-permute-done.refs_0_
  21.5 4.4 %collective-permute-start.1 = (bf16[5,128,128]{2,1,0:T(8,128)(2,1)S(1)}, bf16[5,128,128]{2,1,0:T(8,128)(2,1)S(1)}, u32[]{:S(2)}, u32[]{:S(2)}) collective-permute-start(bf16[5,128,128]{2,1,0:T(8,128)(2,1)S(1)} %slice.52), channel_id=1, source_target_pairs={{0,255},{1,2},{2,1},{3,4},{4,3},{5,6},{6,5},{7,8},{8,7},{9,10},{10... | collective-permute-start | bytes 491528 | tf_op jit(solution)/shard_map/ppermute | solution.py:177
  25.8 0.0 collective-permute-done.10.refs_3_
  25.8 1.3 %collective-permute-start.11 = (bf16[5,128,128]{2,1,0:T(8,128)(2,1)S(1)}, bf16[5,128,128]{2,1,0:T(8,128)(2,1)S(1)}, u32[]{:S(2)}, u32[]{:S(2)}) collective-permute-start(bf16[5,128,128]{2,1,0:T(8,128)(2,1)S(1)} %collective-permute-done.10.refs_3_), channel_id=1, source_target_pairs={{0,31},{1,2},{2,1},{3,4},{4,3},{5,6},{6,5},{7,8},{8,7},{9,10},{10,... | collective-permute-start | bytes 491528 | tf_op jit(solution)/shard_map/ppermute | solution.py:177
  27.2 0.0 collective-permute-done.4.refs_7_
  27.2 0.0 collective-permute-start.5
  27.2 1.3 %collective-permute-done.7.refs_2_ = bf16[5,128,128]{2,1,0:T(8,128)(2,1)S(1)} collective-permute-done((bf16[5,128,128]{2,1,0:T(8,128)(2,1)S(1)}, bf16[5,128,128]{2,1,0:T(8,128)(2,1)S(1)}, u32[]{:S(2)}, u32[]{:S(2)}) %collective-permute-start.7) | collective-permute-done | bytes 163872 | tf_op jit(solution)/shard_map/ppermute | solution.py:178
  28.4 3.8 %collective-permute-start.8 = (bf16[5,128,128]{2,1,0:T(8,128)(2,1)S(1)}, bf16[5,128,128]{2,1,0:T(8,128)(2,1)S(1)}, u32[]{:S(2)}, u32[]{:S(2)}) collective-permute-start(bf16[5,128,128]{2,1,0:T(8,128)(2,1)S(1)} %collective-permute-done.7.refs_2_), channel_id=1, source_target_pairs={{0,255},{1,2},{2,1},{3,4},{4,3},{5,6},{6,5},{7,8},{8,7},{9,10},{10... | collective-permute-start | bytes 491528 | tf_op jit(solution)/shard_map/ppermute | solution.py:177
  32.3 0.0 collective-permute-done.1.refs_6_
  32.3 0.0 collective-permute-start.2
  32.3 0.1 copy.11.pattern
  32.4 1.4 %shard_map.76 = (bf16[2,896,896]{2,1,0:T(8,128)(2,1)S(1)}, bf16[2,128,896]{2,1,0:T(8,128)(2,1)S(1)}, bf16[2,128,896]{2,1,0:T(8,128)(2,1)S(1)}, f32[12,8,128]{2,1,0:T(8,128)S(1)}) custom-call(s32[7,2]{1,0:T(8,128)S(1)} %copy.11.pattern, f32[12]{0:T(128)S(1)} %copy-done.3, bf16[7,2,128,128]{3,2,1,0:T(8,128)(2,1)S(1)} %bitcast.23, ...), custom_call_target="tpu_custom_call" | custom-call | bytes 4194304 | tf_op jit(solution)/shard_map/pallas_call | solution.py:186
  33.8 2.5 %collective-permute-done.11.far1 = bf16[5,128,128]{2,1,0:T(8,128)(2,1)S(1)} collective-permute-done((bf16[5,128,128]{2,1,0:T(8,128)(2,1)S(1)}, bf16[5,128,128]{2,1,0:T(8,128)(2,1)S(1)}, u32[]{:S(2)}, u32[]{:S(2)}) %collective-permute-start.11) | collective-permute-done | bytes 163872 | tf_op jit(solution)/shard_map/ppermute | solution.py:177
  36.3 0.0 collective-permute-done.5.near1
  36.3 3.9 %collective-permute-done.8.far = bf16[5,128,128]{2,1,0:T(8,128)(2,1)S(1)} collective-permute-done((bf16[5,128,128]{2,1,0:T(8,128)(2,1)S(1)}, bf16[5,128,128]{2,1,0:T(8,128)(2,1)S(1)}, u32[]{:S(2)}, u32[]{:S(2)}) %collective-permute-start.8) | collective-permute-done | bytes 163872 | tf_op jit(solution)/shard_map/ppermute | solution.py:177
  40.2 0.0 collective-permute-done.2.near
  40.2 7.2 %shard_map.77 = (f32[7,2,128,128]{3,2,1,0:T(8,128)}, bf16[7,2,128,128]{3,2,1,0:T(8,128)(2,1)}, bf16[7,2,128,128]{3,2,1,0:T(8,128)(2,1)}) custom-call(s32[7,2]{1,0:T(8,128)S(1)} %copy.11.pattern, bf16[5,128,128]{2,1,0:T(8,128)(2,1)S(1)} %collective-permute-done.2.near, bf16[5,128,128]{2,1,0:T(8,128)(2,1)S(1)} %collective-permute-done.5.near1, ...), custom_call_target="tpu_custom_call" | custom-call | flops 3724541952 | bytes 6291456 | tf_op jit(solution)/shard_map/pallas_call | solution.py:206
  (14 shorter events, 0.1 us)
Async XLA Ops:
  0.6 31.6 %copy-start.4 = (s32[7,2,1]{0,2,1:T(1,128)S(1)}, s32[7,2,1]{0,2,1:T(1,128)}, u32[]{:S(2)}) copy-start(s32[7,2,1]{0,2,1:T(1,128)} %param.8) | copy-start | bytes 172
  0.6 31.7 %copy-start = (bf16[7,2,1,128,128]{4,3,2,1,0:T(8,128)(2,1)S(1)}, bf16[7,2,1,128,128]{4,3,2,1,0:T(8,128)(2,1)}, u32[]{:S(2)}) copy-start(bf16[7,2,1,128,128]{4,3,2,1,0:T(8,128)(2,1)} %param.5) | copy-start | bytes 1376260
  0.7 31.7 %copy-start.3 = (f32[12]{0:T(128)S(1)}, f32[12]{0:T(128)}, u32[]{:S(2)}) copy-start(f32[12]{0:T(128)} %weights.1) | copy-start | bytes 148
  0.7 31.7 %copy-start.2 = (bf16[7,2,1,128,128]{4,3,2,1,0:T(8,128)(2,1)S(1)}, bf16[7,2,1,128,128]{4,3,2,1,0:T(8,128)(2,1)}, u32[]{:S(2)}) copy-start(bf16[7,2,1,128,128]{4,3,2,1,0:T(8,128)(2,1)} %param.7) | copy-start | bytes 1376260
  0.7 31.7 %copy-start.1 = (bf16[7,2,1,128,128]{4,3,2,1,0:T(8,128)(2,1)S(1)}, bf16[7,2,1,128,128]{4,3,2,1,0:T(8,128)(2,1)}, u32[]{:S(2)}) copy-start(bf16[7,2,1,128,128]{4,3,2,1,0:T(8,128)(2,1)} %param.6) | copy-start | bytes 1376260
  2.7 14.9 %collective-permute-start.9 = (bf16[6,128,128]{2,1,0:T(8,128)(2,1)S(1)}, bf16[6,128,128]{2,1,0:T(8,128)(2,1)S(1)}, u32[]{:S(2)}, u32[]{:S(2)}) collective-permute-start(bf16[6,128,128]{2,1,0:T(8,128)(2,1)S(1)} %get-tuple-element.20), channel_id=1, source_target_pairs={{0,31},{1,2},{2,1},{3,4},{4,3},{5,6},{6,5},{7,8},{8,7},{9,10},{10,... | collective-permute-start | bytes 589832 | tf_op jit(solution)/shard_map/ppermute | solution.py:177
  11.7 6.1 %collective-permute-start.3 = (bf16[6,128,128]{2,1,0:T(8,128)(2,1)S(1)}, bf16[6,128,128]{2,1,0:T(8,128)(2,1)S(1)}, u32[]{:S(2)}, u32[]{:S(2)}) collective-permute-start(bf16[6,128,128]{2,1,0:T(8,128)(2,1)S(1)} %get-tuple-element.21), channel_id=1, source_target_pairs={{0,1},{1,0},{2,3},{3,2},{4,5},{5,4},{6,7},{7,6},{8,9},{9,8},{10,11... | collective-permute-start | bytes 589832 | tf_op jit(solution)/shard_map/ppermute | solution.py:178
  11.8 9.6 %collective-permute-start.6 = (bf16[6,128,128]{2,1,0:T(8,128)(2,1)S(1)}, bf16[6,128,128]{2,1,0:T(8,128)(2,1)S(1)}, u32[]{:S(2)}, u32[]{:S(2)}) collective-permute-start(bf16[6,128,128]{2,1,0:T(8,128)(2,1)S(1)} %get-tuple-element.22), channel_id=1, source_target_pairs={{0,255},{1,2},{2,1},{3,4},{4,3},{5,6},{6,5},{7,8},{8,7},{9,10},{10... | collective-permute-start | bytes 589832 | tf_op jit(solution)/shard_map/ppermute | solution.py:177
  14.4 7.0 %collective-permute-start = (bf16[6,128,128]{2,1,0:T(8,128)(2,1)S(1)}, bf16[6,128,128]{2,1,0:T(8,128)(2,1)S(1)}, u32[]{:S(2)}, u32[]{:S(2)}) collective-permute-start(bf16[6,128,128]{2,1,0:T(8,128)(2,1)S(1)} %get-tuple-element.23), channel_id=1, source_target_pairs={{0,1},{1,0},{2,3},{3,2},{4,5},{5,4},{6,7},{7,6},{8,9},{9,8},{10,11... | collective-permute-start | bytes 589832 | tf_op jit(solution)/shard_map/ppermute | solution.py:178
  17.7 8.1 %collective-permute-start.10 = (bf16[5,128,128]{2,1,0:T(8,128)(2,1)S(1)}, bf16[5,128,128]{2,1,0:T(8,128)(2,1)S(1)}, u32[]{:S(2)}, u32[]{:S(2)}) collective-permute-start(bf16[5,128,128]{2,1,0:T(8,128)(2,1)S(1)} %slice.57), channel_id=1, source_target_pairs={{0,1},{1,0},{2,3},{3,2},{4,5},{5,4},{6,7},{7,6},{8,9},{9,8},{10,11... | collective-permute-start | bytes 491528 | tf_op jit(solution)/shard_map/ppermute | solution.py:178
  17.8 9.3 %collective-permute-start.4 = (bf16[5,128,128]{2,1,0:T(8,128)(2,1)S(1)}, bf16[5,128,128]{2,1,0:T(8,128)(2,1)S(1)}, u32[]{:S(2)}, u32[]{:S(2)}) collective-permute-start(bf16[5,128,128]{2,1,0:T(8,128)(2,1)S(1)} %slice.55), channel_id=1, source_target_pairs={{0,31},{1,2},{2,1},{3,4},{4,3},{5,6},{6,5},{7,8},{8,7},{9,10},{10,... | collective-permute-start | bytes 491528 | tf_op jit(solution)/shard_map/ppermute | solution.py:177
  21.3 7.1 %collective-permute-start.7 = (bf16[5,128,128]{2,1,0:T(8,128)(2,1)S(1)}, bf16[5,128,128]{2,1,0:T(8,128)(2,1)S(1)}, u32[]{:S(2)}, u32[]{:S(2)}) collective-permute-start(bf16[5,128,128]{2,1,0:T(8,128)(2,1)S(1)} %slice.56), channel_id=1, source_target_pairs={{0,1},{1,0},{2,3},{3,2},{4,5},{5,4},{6,7},{7,6},{8,9},{9,8},{10,11... | collective-permute-start | bytes 491528 | tf_op jit(solution)/shard_map/ppermute | solution.py:178
  21.5 10.8 %collective-permute-start.1 = (bf16[5,128,128]{2,1,0:T(8,128)(2,1)S(1)}, bf16[5,128,128]{2,1,0:T(8,128)(2,1)S(1)}, u32[]{:S(2)}, u32[]{:S(2)}) collective-permute-start(bf16[5,128,128]{2,1,0:T(8,128)(2,1)S(1)} %slice.52), channel_id=1, source_target_pairs={{0,255},{1,2},{2,1},{3,4},{4,3},{5,6},{6,5},{7,8},{8,7},{9,10},{10... | collective-permute-start | bytes 491528 | tf_op jit(solution)/shard_map/ppermute | solution.py:177
  25.8 10.5 %collective-permute-start.11 = (bf16[5,128,128]{2,1,0:T(8,128)(2,1)S(1)}, bf16[5,128,128]{2,1,0:T(8,128)(2,1)S(1)}, u32[]{:S(2)}, u32[]{:S(2)}) collective-permute-start(bf16[5,128,128]{2,1,0:T(8,128)(2,1)S(1)} %collective-permute-done.10.refs_3_), channel_id=1, source_target_pairs={{0,31},{1,2},{2,1},{3,4},{4,3},{5,6},{6,5},{7,8},{8,7},{9,10},{10,... | collective-permute-start | bytes 491528 | tf_op jit(solution)/shard_map/ppermute | solution.py:177
  27.2 9.2 %collective-permute-start.5 = (bf16[5,128,128]{2,1,0:T(8,128)(2,1)S(1)}, bf16[5,128,128]{2,1,0:T(8,128)(2,1)S(1)}, u32[]{:S(2)}, u32[]{:S(2)}) collective-permute-start(bf16[5,128,128]{2,1,0:T(8,128)(2,1)S(1)} %collective-permute-done.4.refs_7_), channel_id=1, source_target_pairs={{0,1},{1,0},{2,3},{3,2},{4,5},{5,4},{6,7},{7,6},{8,9},{9,8},{10,11... | collective-permute-start | bytes 491528 | tf_op jit(solution)/shard_map/ppermute | solution.py:178
  28.4 11.8 %collective-permute-start.8 = (bf16[5,128,128]{2,1,0:T(8,128)(2,1)S(1)}, bf16[5,128,128]{2,1,0:T(8,128)(2,1)S(1)}, u32[]{:S(2)}, u32[]{:S(2)}) collective-permute-start(bf16[5,128,128]{2,1,0:T(8,128)(2,1)S(1)} %collective-permute-done.7.refs_2_), channel_id=1, source_target_pairs={{0,255},{1,2},{2,1},{3,4},{4,3},{5,6},{6,5},{7,8},{8,7},{9,10},{10... | collective-permute-start | bytes 491528 | tf_op jit(solution)/shard_map/ppermute | solution.py:177
  32.3 7.9 %collective-permute-start.2 = (bf16[5,128,128]{2,1,0:T(8,128)(2,1)S(1)}, bf16[5,128,128]{2,1,0:T(8,128)(2,1)S(1)}, u32[]{:S(2)}, u32[]{:S(2)}) collective-permute-start(bf16[5,128,128]{2,1,0:T(8,128)(2,1)S(1)} %collective-permute-done.1.refs_6_), channel_id=1, source_target_pairs={{0,1},{1,0},{2,3},{3,2},{4,5},{5,4},{6,7},{7,6},{8,9},{9,8},{10,11... | collective-permute-start | bytes 491528 | tf_op jit(solution)/shard_map/ppermute | solution.py:178

commit v4 on v3

--- a/solution.py
+++ b/solution.py
@@ -9,7 +9,6 @@
 
 BAND = 3
 TERMS = 12
-LEAST = 5
 GROUPS = ((0, 2), (2, 4), (4, 6), (6, 7))
 
 
@@ -174,8 +173,8 @@
     for dist in range(1, BAND + 1):
         from_far, from_near = [], []
         for slot in range(rows):
-            from_far.append(lax.ppermute(to_far[slot][: max(offsets - dist, LEAST)], axes, across[slot]))
-            from_near.append(lax.ppermute(to_near[slot][: max(offsets - dist, LEAST)], axes, pairs))
+            from_far.append(lax.ppermute(to_far[slot][: offsets - dist], axes, across[slot]))
+            from_near.append(lax.ppermute(to_near[slot][: offsets - dist], axes, pairs))
         near += from_near
         far += from_far
         to_far, to_near = from_near, from_far

time: 47.7 us -> 47.4 us (level); the launches traced: 47.5 us -> 46.7 us
  waiting for transfers between devices: 11.2 us -> 7.68 us
  local copies, waits for them, and re-layouts: 0.18 us -> 2.18 us
  starting transfers between devices: 24.5 us -> 25.2 us
    ppermute x12, waiting for transfers between devices: 11.2 us -> 7.68 us  [the longest x6 7.09 us: body(): lax.ppermute(to_far[slot][:offsets - dist], axes, across[slot])]
    slice x4 -> x8, local copies, waits for them, and re-layouts: 0.05 us -> 2.05 us  [the longest x4 1.35 us: body(): from_near.append(lax.ppermute(to_near[slot][:offsets - dist], axes, pairs))]
    ppermute x12, starting transfers between devices: 24.5 us -> 25.2 us  [the longest x6 25 us: body(): lax.ppermute(to_far[slot][:offsets - dist], axes, across[slot])]
  transfers between devices with their start and end apart: 12 -> 12, of which waited for: 5 -> 4; matrix products, arithmetic and copies ran while one was open for 0% -> 5% of each run, Pallas kernels for 3% -> 3%
where the time goes in v4:
time: 47.4 us; the launch traced here: 46.7 us
  starting transfers between devices  25.2 us (53%)
  Pallas kernels  8.6 us (18%)
  waiting for transfers between devices  7.68 us (16%)
  local copies, waits for them, and re-layouts  2.18 us (5%)
  other arithmetic  2.08 us (4%)
  between operations  0.97 us (2%)
    ppermute x6, starting transfers between devices, body(): lax.ppermute(to_far[slot][:offsets - dist], axes, across[slot])  25 us
    pallas_call x1, Pallas kernels, body(): pl.pallas_call(terms_kernel, out_shape=(jax.ShapeDtypeStruct(band_shape,...  7.19 us
    ppermute x6, waiting for transfers between devices, body(): lax.ppermute(to_far[slot][:offsets - dist], axes, across[slot])  7.09 us
    pallas_call x1, Pallas kernels, body(): pl.pallas_call(start_kernel, out_shape=(table, term, term, jax.ShapeDtype...  1.4 us
    slice x4, local copies, waits for them, and re-layouts, body(): from_near.append(lax.ppermute(to_near[slot][:offsets - dist], axes, pairs))  1.35 us
    mul x1, other arithmetic, body(): kept = ham * live.astype(ham.dtype)[:, :, None, None]  1.11 us
  transfers between devices with their start and end apart: 12, of which 4 were waited for; matrix products, arithmetic and copies ran while one was open for 5% of the time, Pallas kernels for 3%

profile of v4, /device:TPU:1, one launch (start us, length us, event | category | flops | bytes accessed | tf_op | source)
XLA Modules:
  0.0 46.7 jit_solution(14115974625622995414)
XLA Ops:
  0.6 0.0 copy-start
  0.7 0.8 %convert_element_type.7 = bf16[7,2]{0,1:T(2,128)(2,1)S(1)} convert(s32[7,2]{0,1:T(2,128)} %bitcast.26) | non-fusion elementwise | flops 14 | bytes 84 | tf_op jit(solution)/shard_map/convert_element_type | solution.py:164
  1.5 1.1 %bitcast_multiply_fusion = bf16[7,2,128,128]{3,2,0,1:T(8,128)(2,1)S(1)} fusion(bf16[7,2,1,128,128]{4,3,2,1,0:T(8,128)(2,1)} %param.5, bf16[7,2]{0,1:T(2,128)(2,1)S(1)} %convert_element_type.7), kind=kLoop, calls=%fused_computation | loop fusion | flops 229376 | bytes 917532 | tf_op jit(solution)/shard_map/mul | solution.py:164
  2.6 0.1 select_bitcast_fusion
  2.7 9.0 %collective-permute-start.9 = (bf16[6,128,128]{2,1,0:T(8,128)(2,1)S(1)}, bf16[6,128,128]{2,1,0:T(8,128)(2,1)S(1)}, u32[]{:S(2)}, u32[]{:S(2)}) collective-permute-start(bf16[6,128,128]{2,1,0:T(8,128)(2,1)S(1)} %get-tuple-element.20), channel_id=1, source_target_pairs={{0,31},{1,2},{2,1},{3,4},{4,3},{5,6},{6,5},{7,8},{8,7},{9,10},{10,... | collective-permute-start | bytes 589832 | tf_op jit(solution)/shard_map/ppermute | solution.py:176
  11.7 0.0 collective-permute-start.3
  11.7 0.1 select_bitcast_fusion.1
  11.8 2.7 %collective-permute-start.6 = (bf16[6,128,128]{2,1,0:T(8,128)(2,1)S(1)}, bf16[6,128,128]{2,1,0:T(8,128)(2,1)S(1)}, u32[]{:S(2)}, u32[]{:S(2)}) collective-permute-start(bf16[6,128,128]{2,1,0:T(8,128)(2,1)S(1)} %get-tuple-element.22), channel_id=1, source_target_pairs={{0,255},{1,2},{2,1},{3,4},{4,3},{5,6},{6,5},{7,8},{8,7},{9,10},{10... | collective-permute-start | bytes 589832 | tf_op jit(solution)/shard_map/ppermute | solution.py:176
  14.4 0.0 collective-permute-start
  14.4 3.2 %collective-permute-done.9.refs_5_ = bf16[6,128,128]{2,1,0:T(8,128)(2,1)S(1)} collective-permute-done((bf16[6,128,128]{2,1,0:T(8,128)(2,1)S(1)}, bf16[6,128,128]{2,1,0:T(8,128)(2,1)S(1)}, u32[]{:S(2)}, u32[]{:S(2)}) %collective-permute-start.9) | collective-permute-done | bytes 196640 | tf_op jit(solution)/shard_map/ppermute | solution.py:176
  17.7 0.1 collective-permute-start.10
  17.8 0.0 collective-permute-done.3.refs_1_
  17.8 3.2 %collective-permute-start.4 = (bf16[5,128,128]{2,1,0:T(8,128)(2,1)S(1)}, bf16[5,128,128]{2,1,0:T(8,128)(2,1)S(1)}, u32[]{:S(2)}, u32[]{:S(2)}) collective-permute-start(bf16[5,128,128]{2,1,0:T(8,128)(2,1)S(1)} %slice.72), channel_id=1, source_target_pairs={{0,31},{1,2},{2,1},{3,4},{4,3},{5,6},{6,5},{7,8},{8,7},{9,10},{10,... | collective-permute-start | bytes 491528 | tf_op jit(solution)/shard_map/ppermute | solution.py:176
  21.0 0.3 collective-permute-done.6.refs_4_
  21.3 0.1 collective-permute-start.7
  21.4 0.0 collective-permute-done.refs_0_
  21.5 4.4 %collective-permute-start.1 = (bf16[5,128,128]{2,1,0:T(8,128)(2,1)S(1)}, bf16[5,128,128]{2,1,0:T(8,128)(2,1)S(1)}, u32[]{:S(2)}, u32[]{:S(2)}) collective-permute-start(bf16[5,128,128]{2,1,0:T(8,128)(2,1)S(1)} %slice.68), channel_id=1, source_target_pairs={{0,255},{1,2},{2,1},{3,4},{4,3},{5,6},{6,5},{7,8},{8,7},{9,10},{10... | collective-permute-start | bytes 491528 | tf_op jit(solution)/shard_map/ppermute | solution.py:176
  25.9 1.3 %collective-permute-start.11 = (bf16[4,128,128]{2,1,0:T(8,128)(2,1)S(1)}, bf16[4,128,128]{2,1,0:T(8,128)(2,1)S(1)}, u32[]{:S(2)}, u32[]{:S(2)}) collective-permute-start(bf16[4,128,128]{2,1,0:T(8,128)(2,1)S(1)} %slice.77), channel_id=1, source_target_pairs={{0,31},{1,2},{2,1},{3,4},{4,3},{5,6},{6,5},{7,8},{8,7},{9,10},{10,... | collective-permute-start | bytes 393224 | tf_op jit(solution)/shard_map/ppermute | solution.py:176
  27.2 0.0 collective-permute-done.4.refs_7_
  27.2 0.7 %slice.73 = bf16[4,128,128]{2,1,0:T(8,128)(2,1)} slice(bf16[5,128,128]{2,1,0:T(8,128)(2,1)S(1)} %collective-permute-done.4.refs_7_), slice={[0:4], [0:128], [0:128]} | slice | bytes 262144 | tf_op jit(solution)/shard_map/slice | solution.py:177
  27.8 0.0 collective-permute-start.5
  27.8 0.6 %collective-permute-done.7.refs_2_ = bf16[5,128,128]{2,1,0:T(8,128)(2,1)S(1)} collective-permute-done((bf16[5,128,128]{2,1,0:T(8,128)(2,1)S(1)}, bf16[5,128,128]{2,1,0:T(8,128)(2,1)S(1)}, u32[]{:S(2)}, u32[]{:S(2)}) %collective-permute-start.7) | collective-permute-done | bytes 163872 | tf_op jit(solution)/shard_map/ppermute | solution.py:177
  28.4 0.7 %slice.75 = bf16[4,128,128]{2,1,0:T(8,128)(2,1)} slice(bf16[5,128,128]{2,1,0:T(8,128)(2,1)S(1)} %collective-permute-done.7.refs_2_), slice={[0:4], [0:128], [0:128]} | slice | bytes 262144 | tf_op jit(solution)/shard_map/slice | solution.py:176
  29.1 4.5 %collective-permute-start.8 = (bf16[4,128,128]{2,1,0:T(8,128)(2,1)}, bf16[4,128,128]{2,1,0:T(8,128)(2,1)S(1)}, u32[]{:S(2)}, u32[]{:S(2)}) collective-permute-start(bf16[4,128,128]{2,1,0:T(8,128)(2,1)} %slice.75), channel_id=1, source_target_pairs={{0,255},{1,2},{2,1},{3,4},{4,3},{5,6},{6,5},{7,8},{8,7},{9,10},{10... | collective-permute-start | bytes 393224 | tf_op jit(solution)/shard_map/ppermute | solution.py:176
  33.6 0.7 %slice.69 = bf16[4,128,128]{2,1,0:T(8,128)(2,1)} slice(bf16[5,128,128]{2,1,0:T(8,128)(2,1)S(1)} %collective-permute-done.1.refs_6_), slice={[0:4], [0:128], [0:128]} | slice | bytes 262144 | tf_op jit(solution)/shard_map/slice | solution.py:177
  34.3 0.0 collective-permute-start.2
  34.3 0.1 copy.11.pattern
  34.4 1.4 %shard_map.76 = (bf16[2,896,896]{2,1,0:T(8,128)(2,1)S(1)}, bf16[2,128,896]{2,1,0:T(8,128)(2,1)S(1)}, bf16[2,128,896]{2,1,0:T(8,128)(2,1)S(1)}, f32[12,8,128]{2,1,0:T(8,128)S(1)}) custom-call(s32[7,2]{1,0:T(8,128)S(1)} %copy.11.pattern, f32[12]{0:T(128)S(1)} %copy-done.3, bf16[7,2,128,128]{3,2,1,0:T(8,128)(2,1)S(1)} %bitcast.23, ...), custom_call_target="tpu_custom_call" | custom-call | bytes 4194304 | tf_op jit(solution)/shard_map/pallas_call | solution.py:185
  35.8 0.0 collective-permute-done.11.far1
  35.8 3.5 %collective-permute-done.8.far = bf16[4,128,128]{2,1,0:T(8,128)(2,1)S(1)} collective-permute-done((bf16[4,128,128]{2,1,0:T(8,128)(2,1)}, bf16[4,128,128]{2,1,0:T(8,128)(2,1)S(1)}, u32[]{:S(2)}, u32[]{:S(2)}) %collective-permute-start.8) | collective-permute-done | bytes 131104 | tf_op jit(solution)/shard_map/ppermute | solution.py:176
  39.3 0.0 collective-permute-done.2.near
  39.3 7.2 %shard_map.77 = (f32[7,2,128,128]{3,2,1,0:T(8,128)}, bf16[7,2,128,128]{3,2,1,0:T(8,128)(2,1)}, bf16[7,2,128,128]{3,2,1,0:T(8,128)(2,1)}) custom-call(s32[7,2]{1,0:T(8,128)S(1)} %copy.11.pattern, bf16[4,128,128]{2,1,0:T(8,128)(2,1)S(1)} %collective-permute-done.2.near, bf16[4,128,128]{2,1,0:T(8,128)(2,1)S(1)} %collective-permute-done.5.near1, ...), custom_call_target="tpu_custom_call" | custom-call | flops 3724541952 | bytes 6291456 | tf_op jit(solution)/shard_map/pallas_call | solution.py:205
  (18 shorter events, 0.1 us)
Async XLA Ops:
  0.6 33.6 %copy-start.4 = (s32[7,2,1]{0,2,1:T(1,128)S(1)}, s32[7,2,1]{0,2,1:T(1,128)}, u32[]{:S(2)}) copy-start(s32[7,2,1]{0,2,1:T(1,128)} %param.8) | copy-start | bytes 172
  0.6 33.7 %copy-start = (bf16[7,2,1,128,128]{4,3,2,1,0:T(8,128)(2,1)S(1)}, bf16[7,2,1,128,128]{4,3,2,1,0:T(8,128)(2,1)}, u32[]{:S(2)}) copy-start(bf16[7,2,1,128,128]{4,3,2,1,0:T(8,128)(2,1)} %param.5) | copy-start | bytes 1376260
  0.7 33.7 %copy-start.3 = (f32[12]{0:T(128)S(1)}, f32[12]{0:T(128)}, u32[]{:S(2)}) copy-start(f32[12]{0:T(128)} %weights.1) | copy-start | bytes 148
  0.7 33.7 %copy-start.2 = (bf16[7,2,1,128,128]{4,3,2,1,0:T(8,128)(2,1)S(1)}, bf16[7,2,1,128,128]{4,3,2,1,0:T(8,128)(2,1)}, u32[]{:S(2)}) copy-start(bf16[7,2,1,128,128]{4,3,2,1,0:T(8,128)(2,1)} %param.7) | copy-start | bytes 1376260
  0.7 33.7 %copy-start.1 = (bf16[7,2,1,128,128]{4,3,2,1,0:T(8,128)(2,1)S(1)}, bf16[7,2,1,128,128]{4,3,2,1,0:T(8,128)(2,1)}, u32[]{:S(2)}) copy-start(bf16[7,2,1,128,128]{4,3,2,1,0:T(8,128)(2,1)} %param.6) | copy-start | bytes 1376260
  2.7 14.9 %collective-permute-start.9 = (bf16[6,128,128]{2,1,0:T(8,128)(2,1)S(1)}, bf16[6,128,128]{2,1,0:T(8,128)(2,1)S(1)}, u32[]{:S(2)}, u32[]{:S(2)}) collective-permute-start(bf16[6,128,128]{2,1,0:T(8,128)(2,1)S(1)} %get-tuple-element.20), channel_id=1, source_target_pairs={{0,31},{1,2},{2,1},{3,4},{4,3},{5,6},{6,5},{7,8},{8,7},{9,10},{10,... | collective-permute-start | bytes 589832 | tf_op jit(solution)/shard_map/ppermute | solution.py:176
  11.7 6.1 %collective-permute-start.3 = (bf16[6,128,128]{2,1,0:T(8,128)(2,1)S(1)}, bf16[6,128,128]{2,1,0:T(8,128)(2,1)S(1)}, u32[]{:S(2)}, u32[]{:S(2)}) collective-permute-start(bf16[6,128,128]{2,1,0:T(8,128)(2,1)S(1)} %get-tuple-element.21), channel_id=1, source_target_pairs={{0,1},{1,0},{2,3},{3,2},{4,5},{5,4},{6,7},{7,6},{8,9},{9,8},{10,11... | collective-permute-start | bytes 589832 | tf_op jit(solution)/shard_map/ppermute | solution.py:177
  11.8 9.6 %collective-permute-start.6 = (bf16[6,128,128]{2,1,0:T(8,128)(2,1)S(1)}, bf16[6,128,128]{2,1,0:T(8,128)(2,1)S(1)}, u32[]{:S(2)}, u32[]{:S(2)}) collective-permute-start(bf16[6,128,128]{2,1,0:T(8,128)(2,1)S(1)} %get-tuple-element.22), channel_id=1, source_target_pairs={{0,255},{1,2},{2,1},{3,4},{4,3},{5,6},{6,5},{7,8},{8,7},{9,10},{10... | collective-permute-start | bytes 589832 | tf_op jit(solution)/shard_map/ppermute | solution.py:176
  14.4 7.0 %collective-permute-start = (bf16[6,128,128]{2,1,0:T(8,128)(2,1)S(1)}, bf16[6,128,128]{2,1,0:T(8,128)(2,1)S(1)}, u32[]{:S(2)}, u32[]{:S(2)}) collective-permute-start(bf16[6,128,128]{2,1,0:T(8,128)(2,1)S(1)} %get-tuple-element.23), channel_id=1, source_target_pairs={{0,1},{1,0},{2,3},{3,2},{4,5},{5,4},{6,7},{7,6},{8,9},{9,8},{10,11... | collective-permute-start | bytes 589832 | tf_op jit(solution)/shard_map/ppermute | solution.py:177
  17.7 8.1 %collective-permute-start.10 = (bf16[5,128,128]{2,1,0:T(8,128)(2,1)S(1)}, bf16[5,128,128]{2,1,0:T(8,128)(2,1)S(1)}, u32[]{:S(2)}, u32[]{:S(2)}) collective-permute-start(bf16[5,128,128]{2,1,0:T(8,128)(2,1)S(1)} %slice.76), channel_id=1, source_target_pairs={{0,1},{1,0},{2,3},{3,2},{4,5},{5,4},{6,7},{7,6},{8,9},{9,8},{10,11... | collective-permute-start | bytes 491528 | tf_op jit(solution)/shard_map/ppermute | solution.py:177
  17.8 9.3 %collective-permute-start.4 = (bf16[5,128,128]{2,1,0:T(8,128)(2,1)S(1)}, bf16[5,128,128]{2,1,0:T(8,128)(2,1)S(1)}, u32[]{:S(2)}, u32[]{:S(2)}) collective-permute-start(bf16[5,128,128]{2,1,0:T(8,128)(2,1)S(1)} %slice.72), channel_id=1, source_target_pairs={{0,31},{1,2},{2,1},{3,4},{4,3},{5,6},{6,5},{7,8},{8,7},{9,10},{10,... | collective-permute-start | bytes 491528 | tf_op jit(solution)/shard_map/ppermute | solution.py:176
  21.3 7.1 %collective-permute-start.7 = (bf16[5,128,128]{2,1,0:T(8,128)(2,1)S(1)}, bf16[5,128,128]{2,1,0:T(8,128)(2,1)S(1)}, u32[]{:S(2)}, u32[]{:S(2)}) collective-permute-start(bf16[5,128,128]{2,1,0:T(8,128)(2,1)S(1)} %slice.74), channel_id=1, source_target_pairs={{0,1},{1,0},{2,3},{3,2},{4,5},{5,4},{6,7},{7,6},{8,9},{9,8},{10,11... | collective-permute-start | bytes 491528 | tf_op jit(solution)/shard_map/ppermute | solution.py:177
  21.5 12.1 %collective-permute-start.1 = (bf16[5,128,128]{2,1,0:T(8,128)(2,1)S(1)}, bf16[5,128,128]{2,1,0:T(8,128)(2,1)S(1)}, u32[]{:S(2)}, u32[]{:S(2)}) collective-permute-start(bf16[5,128,128]{2,1,0:T(8,128)(2,1)S(1)} %slice.68), channel_id=1, source_target_pairs={{0,255},{1,2},{2,1},{3,4},{4,3},{5,6},{6,5},{7,8},{8,7},{9,10},{10... | collective-permute-start | bytes 491528 | tf_op jit(solution)/shard_map/ppermute | solution.py:176
  25.9 9.9 %collective-permute-start.11 = (bf16[4,128,128]{2,1,0:T(8,128)(2,1)S(1)}, bf16[4,128,128]{2,1,0:T(8,128)(2,1)S(1)}, u32[]{:S(2)}, u32[]{:S(2)}) collective-permute-start(bf16[4,128,128]{2,1,0:T(8,128)(2,1)S(1)} %slice.77), channel_id=1, source_target_pairs={{0,31},{1,2},{2,1},{3,4},{4,3},{5,6},{6,5},{7,8},{8,7},{9,10},{10,... | collective-permute-start | bytes 393224 | tf_op jit(solution)/shard_map/ppermute | solution.py:176
  27.8 8.0 %collective-permute-start.5 = (bf16[4,128,128]{2,1,0:T(8,128)(2,1)}, bf16[4,128,128]{2,1,0:T(8,128)(2,1)S(1)}, u32[]{:S(2)}, u32[]{:S(2)}) collective-permute-start(bf16[4,128,128]{2,1,0:T(8,128)(2,1)} %slice.73), channel_id=1, source_target_pairs={{0,1},{1,0},{2,3},{3,2},{4,5},{5,4},{6,7},{7,6},{8,9},{9,8},{10,11... | collective-permute-start | bytes 393224 | tf_op jit(solution)/shard_map/ppermute | solution.py:177
  29.1 10.3 %collective-permute-start.8 = (bf16[4,128,128]{2,1,0:T(8,128)(2,1)}, bf16[4,128,128]{2,1,0:T(8,128)(2,1)S(1)}, u32[]{:S(2)}, u32[]{:S(2)}) collective-permute-start(bf16[4,128,128]{2,1,0:T(8,128)(2,1)} %slice.75), channel_id=1, source_target_pairs={{0,255},{1,2},{2,1},{3,4},{4,3},{5,6},{6,5},{7,8},{8,7},{9,10},{10... | collective-permute-start | bytes 393224 | tf_op jit(solution)/shard_map/ppermute | solution.py:176
  34.3 5.1 %collective-permute-start.2 = (bf16[4,128,128]{2,1,0:T(8,128)(2,1)}, bf16[4,128,128]{2,1,0:T(8,128)(2,1)S(1)}, u32[]{:S(2)}, u32[]{:S(2)}) collective-permute-start(bf16[4,128,128]{2,1,0:T(8,128)(2,1)} %slice.69), channel_id=1, source_target_pairs={{0,1},{1,0},{2,3},{3,2},{4,5},{5,4},{6,7},{7,6},{8,9},{9,8},{10,11... | collective-permute-start | bytes 393224 | tf_op jit(solution)/shard_map/ppermute | solution.py:177

commit v5 on v4

--- a/solution.py
+++ b/solution.py
@@ -91,8 +91,6 @@
 
 def terms_kernel(pattern, near, near1, far, far1, tiles, table_in, older_in, newer_in, *refs):
     density, out_before, out_last, table, older, newer, total, out_sems = refs
-    older[...] = older_in[...]
-    newer[...] = newer_in[...]
     offsets, rows, block = total.shape[:3]
     stored = mirror(offsets)
     live = alive(pattern)
@@ -101,6 +99,8 @@
         return slice(o * block, (o + 1) * block)
 
     def fill(row):
+        older[row] = older_in[row]
+        newer[row] = newer_in[row]
         for a, start, stop in ((1, 0, 6), (2, 0, 6), (3, 0, 7), (4, 0, 7), (5, 2, 7)):
             part = (row, cols(a), slice(start * block, stop * block))
             table[part] = table_in[part]

time: 47.4 us -> 47.4 us (level)
  no operation moved by 1% of the time
where the time goes in v5:
time: 47.4 us; the launch traced here: 46.7 us
  starting transfers between devices  25.2 us (53%)
  Pallas kernels  8.6 us (18%)
  waiting for transfers between devices  7.68 us (16%)
  local copies, waits for them, and re-layouts  2.18 us (5%)
  other arithmetic  2.08 us (4%)
  between operations  0.97 us (2%)
    ppermute x6, starting transfers between devices, body(): lax.ppermute(to_far[slot][:offsets - dist], axes, across[slot])  25 us
    pallas_call x1, Pallas kernels, body(): pl.pallas_call(terms_kernel, out_shape=(jax.ShapeDtypeStruct(band_shape,...  7.19 us
    ppermute x6, waiting for transfers between devices, body(): lax.ppermute(to_far[slot][:offsets - dist], axes, across[slot])  7.09 us
    pallas_call x1, Pallas kernels, body(): pl.pallas_call(start_kernel, out_shape=(table, term, term, jax.ShapeDtype...  1.4 us
    slice x4, local copies, waits for them, and re-layouts, body(): from_near.append(lax.ppermute(to_near[slot][:offsets - dist], axes, pairs))  1.35 us
    mul x1, other arithmetic, body(): kept = ham * live.astype(ham.dtype)[:, :, None, None]  1.11 us
  transfers between devices with their start and end apart: 12, of which 4 were waited for; matrix products, arithmetic and copies ran while one was open for 5% of the time, Pallas kernels for 3%

profile of v5, /device:TPU:1, one launch (start us, length us, event | category | flops | bytes accessed | tf_op | source)
XLA Modules:
  0.0 46.7 jit_solution(14115974625622995414)
XLA Ops:
  0.6 0.0 copy-start
  0.7 0.8 %convert_element_type.7 = bf16[7,2]{0,1:T(2,128)(2,1)S(1)} convert(s32[7,2]{0,1:T(2,128)} %bitcast.26) | non-fusion elementwise | flops 14 | bytes 84 | tf_op jit(solution)/shard_map/convert_element_type | solution.py:164
  1.5 1.1 %bitcast_multiply_fusion = bf16[7,2,128,128]{3,2,0,1:T(8,128)(2,1)S(1)} fusion(bf16[7,2,1,128,128]{4,3,2,1,0:T(8,128)(2,1)} %param.5, bf16[7,2]{0,1:T(2,128)(2,1)S(1)} %convert_element_type.7), kind=kLoop, calls=%fused_computation | loop fusion | flops 229376 | bytes 917532 | tf_op jit(solution)/shard_map/mul | solution.py:164
  2.6 0.1 select_bitcast_fusion
  2.7 9.0 %collective-permute-start.9 = (bf16[6,128,128]{2,1,0:T(8,128)(2,1)S(1)}, bf16[6,128,128]{2,1,0:T(8,128)(2,1)S(1)}, u32[]{:S(2)}, u32[]{:S(2)}) collective-permute-start(bf16[6,128,128]{2,1,0:T(8,128)(2,1)S(1)} %get-tuple-element.20), channel_id=1, source_target_pairs={{0,31},{1,2},{2,1},{3,4},{4,3},{5,6},{6,5},{7,8},{8,7},{9,10},{10,... | collective-permute-start | bytes 589832 | tf_op jit(solution)/shard_map/ppermute | solution.py:176
  11.7 0.0 collective-permute-start.3
  11.7 0.1 select_bitcast_fusion.1
  11.8 2.7 %collective-permute-start.6 = (bf16[6,128,128]{2,1,0:T(8,128)(2,1)S(1)}, bf16[6,128,128]{2,1,0:T(8,128)(2,1)S(1)}, u32[]{:S(2)}, u32[]{:S(2)}) collective-permute-start(bf16[6,128,128]{2,1,0:T(8,128)(2,1)S(1)} %get-tuple-element.22), channel_id=1, source_target_pairs={{0,255},{1,2},{2,1},{3,4},{4,3},{5,6},{6,5},{7,8},{8,7},{9,10},{10... | collective-permute-start | bytes 589832 | tf_op jit(solution)/shard_map/ppermute | solution.py:176
  14.4 0.0 collective-permute-start
  14.4 3.2 %collective-permute-done.9.refs_5_ = bf16[6,128,128]{2,1,0:T(8,128)(2,1)S(1)} collective-permute-done((bf16[6,128,128]{2,1,0:T(8,128)(2,1)S(1)}, bf16[6,128,128]{2,1,0:T(8,128)(2,1)S(1)}, u32[]{:S(2)}, u32[]{:S(2)}) %collective-permute-start.9) | collective-permute-done | bytes 196640 | tf_op jit(solution)/shard_map/ppermute | solution.py:176
  17.7 0.1 collective-permute-start.10
  17.8 0.0 collective-permute-done.3.refs_1_
  17.8 3.2 %collective-permute-start.4 = (bf16[5,128,128]{2,1,0:T(8,128)(2,1)S(1)}, bf16[5,128,128]{2,1,0:T(8,128)(2,1)S(1)}, u32[]{:S(2)}, u32[]{:S(2)}) collective-permute-start(bf16[5,128,128]{2,1,0:T(8,128)(2,1)S(1)} %slice.72), channel_id=1, source_target_pairs={{0,31},{1,2},{2,1},{3,4},{4,3},{5,6},{6,5},{7,8},{8,7},{9,10},{10,... | collective-permute-start | bytes 491528 | tf_op jit(solution)/shard_map/ppermute | solution.py:176
  21.0 0.3 collective-permute-done.6.refs_4_
  21.3 0.1 collective-permute-start.7
  21.4 0.0 collective-permute-done.refs_0_
  21.5 4.4 %collective-permute-start.1 = (bf16[5,128,128]{2,1,0:T(8,128)(2,1)S(1)}, bf16[5,128,128]{2,1,0:T(8,128)(2,1)S(1)}, u32[]{:S(2)}, u32[]{:S(2)}) collective-permute-start(bf16[5,128,128]{2,1,0:T(8,128)(2,1)S(1)} %slice.68), channel_id=1, source_target_pairs={{0,255},{1,2},{2,1},{3,4},{4,3},{5,6},{6,5},{7,8},{8,7},{9,10},{10... | collective-permute-start | bytes 491528 | tf_op jit(solution)/shard_map/ppermute | solution.py:176
  25.9 1.3 %collective-permute-start.11 = (bf16[4,128,128]{2,1,0:T(8,128)(2,1)S(1)}, bf16[4,128,128]{2,1,0:T(8,128)(2,1)S(1)}, u32[]{:S(2)}, u32[]{:S(2)}) collective-permute-start(bf16[4,128,128]{2,1,0:T(8,128)(2,1)S(1)} %slice.77), channel_id=1, source_target_pairs={{0,31},{1,2},{2,1},{3,4},{4,3},{5,6},{6,5},{7,8},{8,7},{9,10},{10,... | collective-permute-start | bytes 393224 | tf_op jit(solution)/shard_map/ppermute | solution.py:176
  27.2 0.0 collective-permute-done.4.refs_7_
  27.2 0.7 %slice.73 = bf16[4,128,128]{2,1,0:T(8,128)(2,1)} slice(bf16[5,128,128]{2,1,0:T(8,128)(2,1)S(1)} %collective-permute-done.4.refs_7_), slice={[0:4], [0:128], [0:128]} | slice | bytes 262144 | tf_op jit(solution)/shard_map/slice | solution.py:177
  27.8 0.0 collective-permute-start.5
  27.8 0.6 %collective-permute-done.7.refs_2_ = bf16[5,128,128]{2,1,0:T(8,128)(2,1)S(1)} collective-permute-done((bf16[5,128,128]{2,1,0:T(8,128)(2,1)S(1)}, bf16[5,128,128]{2,1,0:T(8,128)(2,1)S(1)}, u32[]{:S(2)}, u32[]{:S(2)}) %collective-permute-start.7) | collective-permute-done | bytes 163872 | tf_op jit(solution)/shard_map/ppermute | solution.py:177
  28.4 0.7 %slice.75 = bf16[4,128,128]{2,1,0:T(8,128)(2,1)} slice(bf16[5,128,128]{2,1,0:T(8,128)(2,1)S(1)} %collective-permute-done.7.refs_2_), slice={[0:4], [0:128], [0:128]} | slice | bytes 262144 | tf_op jit(solution)/shard_map/slice | solution.py:176
  29.1 4.5 %collective-permute-start.8 = (bf16[4,128,128]{2,1,0:T(8,128)(2,1)}, bf16[4,128,128]{2,1,0:T(8,128)(2,1)S(1)}, u32[]{:S(2)}, u32[]{:S(2)}) collective-permute-start(bf16[4,128,128]{2,1,0:T(8,128)(2,1)} %slice.75), channel_id=1, source_target_pairs={{0,255},{1,2},{2,1},{3,4},{4,3},{5,6},{6,5},{7,8},{8,7},{9,10},{10... | collective-permute-start | bytes 393224 | tf_op jit(solution)/shard_map/ppermute | solution.py:176
  33.6 0.7 %slice.69 = bf16[4,128,128]{2,1,0:T(8,128)(2,1)} slice(bf16[5,128,128]{2,1,0:T(8,128)(2,1)S(1)} %collective-permute-done.1.refs_6_), slice={[0:4], [0:128], [0:128]} | slice | bytes 262144 | tf_op jit(solution)/shard_map/slice | solution.py:177
  34.3 0.0 collective-permute-start.2
  34.3 0.1 copy.11.pattern
  34.4 1.4 %shard_map.76 = (bf16[2,896,896]{2,1,0:T(8,128)(2,1)S(1)}, bf16[2,128,896]{2,1,0:T(8,128)(2,1)S(1)}, bf16[2,128,896]{2,1,0:T(8,128)(2,1)S(1)}, f32[12,8,128]{2,1,0:T(8,128)S(1)}) custom-call(s32[7,2]{1,0:T(8,128)S(1)} %copy.11.pattern, f32[12]{0:T(128)S(1)} %copy-done.3, bf16[7,2,128,128]{3,2,1,0:T(8,128)(2,1)S(1)} %bitcast.23, ...), custom_call_target="tpu_custom_call" | custom-call | bytes 4194304 | tf_op jit(solution)/shard_map/pallas_call | solution.py:185
  35.8 0.0 collective-permute-done.11.far1
  35.8 3.5 %collective-permute-done.8.far = bf16[4,128,128]{2,1,0:T(8,128)(2,1)S(1)} collective-permute-done((bf16[4,128,128]{2,1,0:T(8,128)(2,1)}, bf16[4,128,128]{2,1,0:T(8,128)(2,1)S(1)}, u32[]{:S(2)}, u32[]{:S(2)}) %collective-permute-start.8) | collective-permute-done | bytes 131104 | tf_op jit(solution)/shard_map/ppermute | solution.py:176
  39.3 0.0 collective-permute-done.2.near
  39.3 7.2 %shard_map.77 = (f32[7,2,128,128]{3,2,1,0:T(8,128)}, bf16[7,2,128,128]{3,2,1,0:T(8,128)(2,1)}, bf16[7,2,128,128]{3,2,1,0:T(8,128)(2,1)}) custom-call(s32[7,2]{1,0:T(8,128)S(1)} %copy.11.pattern, bf16[4,128,128]{2,1,0:T(8,128)(2,1)S(1)} %collective-permute-done.2.near, bf16[4,128,128]{2,1,0:T(8,128)(2,1)S(1)} %collective-permute-done.5.near1, ...), custom_call_target="tpu_custom_call" | custom-call | flops 3724541952 | bytes 6291456 | tf_op jit(solution)/shard_map/pallas_call | solution.py:205
  (18 shorter events, 0.1 us)
Async XLA Ops:
  0.6 33.6 %copy-start.4 = (s32[7,2,1]{0,2,1:T(1,128)S(1)}, s32[7,2,1]{0,2,1:T(1,128)}, u32[]{:S(2)}) copy-start(s32[7,2,1]{0,2,1:T(1,128)} %param.8) | copy-start | bytes 172
  0.6 33.7 %copy-start = (bf16[7,2,1,128,128]{4,3,2,1,0:T(8,128)(2,1)S(1)}, bf16[7,2,1,128,128]{4,3,2,1,0:T(8,128)(2,1)}, u32[]{:S(2)}) copy-start(bf16[7,2,1,128,128]{4,3,2,1,0:T(8,128)(2,1)} %param.5) | copy-start | bytes 1376260
  0.7 33.7 %copy-start.3 = (f32[12]{0:T(128)S(1)}, f32[12]{0:T(128)}, u32[]{:S(2)}) copy-start(f32[12]{0:T(128)} %weights.1) | copy-start | bytes 148
  0.7 33.7 %copy-start.2 = (bf16[7,2,1,128,128]{4,3,2,1,0:T(8,128)(2,1)S(1)}, bf16[7,2,1,128,128]{4,3,2,1,0:T(8,128)(2,1)}, u32[]{:S(2)}) copy-start(bf16[7,2,1,128,128]{4,3,2,1,0:T(8,128)(2,1)} %param.7) | copy-start | bytes 1376260
  0.7 33.7 %copy-start.1 = (bf16[7,2,1,128,128]{4,3,2,1,0:T(8,128)(2,1)S(1)}, bf16[7,2,1,128,128]{4,3,2,1,0:T(8,128)(2,1)}, u32[]{:S(2)}) copy-start(bf16[7,2,1,128,128]{4,3,2,1,0:T(8,128)(2,1)} %param.6) | copy-start | bytes 1376260
  2.7 14.9 %collective-permute-start.9 = (bf16[6,128,128]{2,1,0:T(8,128)(2,1)S(1)}, bf16[6,128,128]{2,1,0:T(8,128)(2,1)S(1)}, u32[]{:S(2)}, u32[]{:S(2)}) collective-permute-start(bf16[6,128,128]{2,1,0:T(8,128)(2,1)S(1)} %get-tuple-element.20), channel_id=1, source_target_pairs={{0,31},{1,2},{2,1},{3,4},{4,3},{5,6},{6,5},{7,8},{8,7},{9,10},{10,... | collective-permute-start | bytes 589832 | tf_op jit(solution)/shard_map/ppermute | solution.py:176
  11.7 6.1 %collective-permute-start.3 = (bf16[6,128,128]{2,1,0:T(8,128)(2,1)S(1)}, bf16[6,128,128]{2,1,0:T(8,128)(2,1)S(1)}, u32[]{:S(2)}, u32[]{:S(2)}) collective-permute-start(bf16[6,128,128]{2,1,0:T(8,128)(2,1)S(1)} %get-tuple-element.21), channel_id=1, source_target_pairs={{0,1},{1,0},{2,3},{3,2},{4,5},{5,4},{6,7},{7,6},{8,9},{9,8},{10,11... | collective-permute-start | bytes 589832 | tf_op jit(solution)/shard_map/ppermute | solution.py:177
  11.8 9.6 %collective-permute-start.6 = (bf16[6,128,128]{2,1,0:T(8,128)(2,1)S(1)}, bf16[6,128,128]{2,1,0:T(8,128)(2,1)S(1)}, u32[]{:S(2)}, u32[]{:S(2)}) collective-permute-start(bf16[6,128,128]{2,1,0:T(8,128)(2,1)S(1)} %get-tuple-element.22), channel_id=1, source_target_pairs={{0,255},{1,2},{2,1},{3,4},{4,3},{5,6},{6,5},{7,8},{8,7},{9,10},{10... | collective-permute-start | bytes 589832 | tf_op jit(solution)/shard_map/ppermute | solution.py:176
  14.4 7.0 %collective-permute-start = (bf16[6,128,128]{2,1,0:T(8,128)(2,1)S(1)}, bf16[6,128,128]{2,1,0:T(8,128)(2,1)S(1)}, u32[]{:S(2)}, u32[]{:S(2)}) collective-permute-start(bf16[6,128,128]{2,1,0:T(8,128)(2,1)S(1)} %get-tuple-element.23), channel_id=1, source_target_pairs={{0,1},{1,0},{2,3},{3,2},{4,5},{5,4},{6,7},{7,6},{8,9},{9,8},{10,11... | collective-permute-start | bytes 589832 | tf_op jit(solution)/shard_map/ppermute | solution.py:177
  17.7 8.1 %collective-permute-start.10 = (bf16[5,128,128]{2,1,0:T(8,128)(2,1)S(1)}, bf16[5,128,128]{2,1,0:T(8,128)(2,1)S(1)}, u32[]{:S(2)}, u32[]{:S(2)}) collective-permute-start(bf16[5,128,128]{2,1,0:T(8,128)(2,1)S(1)} %slice.76), channel_id=1, source_target_pairs={{0,1},{1,0},{2,3},{3,2},{4,5},{5,4},{6,7},{7,6},{8,9},{9,8},{10,11... | collective-permute-start | bytes 491528 | tf_op jit(solution)/shard_map/ppermute | solution.py:177
  17.8 9.3 %collective-permute-start.4 = (bf16[5,128,128]{2,1,0:T(8,128)(2,1)S(1)}, bf16[5,128,128]{2,1,0:T(8,128)(2,1)S(1)}, u32[]{:S(2)}, u32[]{:S(2)}) collective-permute-start(bf16[5,128,128]{2,1,0:T(8,128)(2,1)S(1)} %slice.72), channel_id=1, source_target_pairs={{0,31},{1,2},{2,1},{3,4},{4,3},{5,6},{6,5},{7,8},{8,7},{9,10},{10,... | collective-permute-start | bytes 491528 | tf_op jit(solution)/shard_map/ppermute | solution.py:176
  21.3 7.1 %collective-permute-start.7 = (bf16[5,128,128]{2,1,0:T(8,128)(2,1)S(1)}, bf16[5,128,128]{2,1,0:T(8,128)(2,1)S(1)}, u32[]{:S(2)}, u32[]{:S(2)}) collective-permute-start(bf16[5,128,128]{2,1,0:T(8,128)(2,1)S(1)} %slice.74), channel_id=1, source_target_pairs={{0,1},{1,0},{2,3},{3,2},{4,5},{5,4},{6,7},{7,6},{8,9},{9,8},{10,11... | collective-permute-start | bytes 491528 | tf_op jit(solution)/shard_map/ppermute | solution.py:177
  21.5 12.1 %collective-permute-start.1 = (bf16[5,128,128]{2,1,0:T(8,128)(2,1)S(1)}, bf16[5,128,128]{2,1,0:T(8,128)(2,1)S(1)}, u32[]{:S(2)}, u32[]{:S(2)}) collective-permute-start(bf16[5,128,128]{2,1,0:T(8,128)(2,1)S(1)} %slice.68), channel_id=1, source_target_pairs={{0,255},{1,2},{2,1},{3,4},{4,3},{5,6},{6,5},{7,8},{8,7},{9,10},{10... | collective-permute-start | bytes 491528 | tf_op jit(solution)/shard_map/ppermute | solution.py:176
  25.9 9.9 %collective-permute-start.11 = (bf16[4,128,128]{2,1,0:T(8,128)(2,1)S(1)}, bf16[4,128,128]{2,1,0:T(8,128)(2,1)S(1)}, u32[]{:S(2)}, u32[]{:S(2)}) collective-permute-start(bf16[4,128,128]{2,1,0:T(8,128)(2,1)S(1)} %slice.77), channel_id=1, source_target_pairs={{0,31},{1,2},{2,1},{3,4},{4,3},{5,6},{6,5},{7,8},{8,7},{9,10},{10,... | collective-permute-start | bytes 393224 | tf_op jit(solution)/shard_map/ppermute | solution.py:176
  27.8 8.0 %collective-permute-start.5 = (bf16[4,128,128]{2,1,0:T(8,128)(2,1)}, bf16[4,128,128]{2,1,0:T(8,128)(2,1)S(1)}, u32[]{:S(2)}, u32[]{:S(2)}) collective-permute-start(bf16[4,128,128]{2,1,0:T(8,128)(2,1)} %slice.73), channel_id=1, source_target_pairs={{0,1},{1,0},{2,3},{3,2},{4,5},{5,4},{6,7},{7,6},{8,9},{9,8},{10,11... | collective-permute-start | bytes 393224 | tf_op jit(solution)/shard_map/ppermute | solution.py:177
  29.1 10.3 %collective-permute-start.8 = (bf16[4,128,128]{2,1,0:T(8,128)(2,1)}, bf16[4,128,128]{2,1,0:T(8,128)(2,1)S(1)}, u32[]{:S(2)}, u32[]{:S(2)}) collective-permute-start(bf16[4,128,128]{2,1,0:T(8,128)(2,1)} %slice.75), channel_id=1, source_target_pairs={{0,255},{1,2},{2,1},{3,4},{4,3},{5,6},{6,5},{7,8},{8,7},{9,10},{10... | collective-permute-start | bytes 393224 | tf_op jit(solution)/shard_map/ppermute | solution.py:176
  34.3 5.1 %collective-permute-start.2 = (bf16[4,128,128]{2,1,0:T(8,128)(2,1)}, bf16[4,128,128]{2,1,0:T(8,128)(2,1)S(1)}, u32[]{:S(2)}, u32[]{:S(2)}) collective-permute-start(bf16[4,128,128]{2,1,0:T(8,128)(2,1)} %slice.69), channel_id=1, source_target_pairs={{0,1},{1,0},{2,3},{3,2},{4,5},{5,4},{6,7},{7,6},{8,9},{9,8},{10,11... | collective-permute-start | bytes 393224 | tf_op jit(solution)/shard_map/ppermute | solution.py:177
